TPU v7x, 32 devices: a whole 2x2x4 slice. The times are simulated.
32 devices in a mesh: dp: 8 (over y, x, core), mp: 4 (over z).
Axes of the slice: x: 2, y: 2, z: 4, core: 2. Of those that a mesh axis runs over, the one named last changes fastest.
Arguments:
- inputs: bfloat16 [16384, 768], P('dp'), may hold values from -6 to 6
- cotangent: bfloat16 [16384, 768], P('dp'), may hold values from -6 to 6
- span_table: int32 [32, 2], P('dp'), may hold values from 0 to 486, as said below
- ln1_gain: bfloat16 [768], replicated, may hold values from 0.5 to 1.5
- ln1_shift: bfloat16 [768], replicated, may hold values from -2 to 2
- w_query: bfloat16 [768, 768], P(None, 'mp'), may hold values from -0.21875 to 0.21875
- b_query: bfloat16 [768], P('mp'), may hold values from -2 to 2
- w_key: bfloat16 [768, 768], P(None, 'mp'), may hold values from -0.21875 to 0.21875
- w_value: bfloat16 [768, 768], P(None, 'mp'), may hold values from -0.21875 to 0.21875
- b_value: bfloat16 [768], P('mp'), may hold values from -2 to 2
- w_out: bfloat16 [768, 768], P('mp'), may hold values from -0.875 to 0.875
- b_out: bfloat16 [768], replicated, may hold values from -2 to 2
- ln2_gain: bfloat16 [768], replicated, may hold values from 0.5 to 1.5
- ln2_shift: bfloat16 [768], replicated, may hold values from -2 to 2
- w_up: bfloat16 [768, 3072], P(None, 'mp'), may hold values from -0.21875 to 0.21875
- b_up: bfloat16 [3072], P('mp'), may hold values from -2 to 2
- w_down: bfloat16 [3072, 768], P('mp'), may hold values from -0.109375 to 0.109375
- b_down: bfloat16 [768], replicated, may hold values from -2 to 2
Outputs:
- layer_out: bfloat16 [16384, 768], P(('dp', 'mp'))
- grad_inputs: bfloat16 [16384, 768], P(('dp', 'mp'))
- grad_ln1_gain: float32 [768], replicated
- grad_ln1_shift: float32 [768], replicated
- grad_w_query: float32 [768, 768], P(None, 'mp')
- grad_b_query: float32 [768], P('mp')
- grad_w_key: float32 [768, 768], P(None, 'mp')
- grad_w_value: float32 [768, 768], P(None, 'mp')
- grad_b_value: float32 [768], P('mp')
- grad_w_out: float32 [768, 768], P('mp')
- grad_b_out: float32 [768], replicated
- grad_ln2_gain: float32 [768], replicated
- grad_ln2_shift: float32 [768], replicated
- grad_w_up: float32 [768, 3072], P(None, 'mp')
- grad_b_up: float32 [3072], P('mp')
- grad_w_down: float32 [3072, 768], P('mp')
- grad_b_down: float32 [768], replicated
Inputs may be any that keep to these rules, and one draw needn't show every extreme that they name: `span_table`: column 0 is the first masked position and column 1 the number of masked positions, between 26 and 128; each span lies inside its sequence; both extreme lengths occur.
All inputs are finite; a program needn't handle non-finite values.
Results may differ from a plain program's by a relative error of at most 0.019.
Values may be sent and summed in bfloat16 or wider, within the bound.
No kernel may reach another device: no remote copies, remote signals or barrier semaphores. Data moves between devices by JAX's collectives and lax.ppermute only.
A program may use at most 192 MiB of HBM per device.

v0:
```python
import jax
import jax.numpy as jnp
from jax import lax
from jax.sharding import PartitionSpec as P

HD = 64


norm_eps = 1e-06


def matmul(left, right):
    return jnp.dot(left, right, preferred_element_type=jnp.float32)


def matmul_tn(left, right):
    return lax.dot_general(
        left, right, (((0,), (0,)), ((), ())), preferred_element_type=jnp.float32
    )


def matmul_nt(left, right):
    return lax.dot_general(
        left, right, (((1,), (1,)), ((), ())), preferred_element_type=jnp.float32
    )


def normalize(values, gain, shift):
    centered = values - jnp.mean(values, -1, keepdims=True)
    rstd_rows = lax.rsqrt(jnp.mean(centered * centered, -1, keepdims=True) + norm_eps)
    unit_rows = centered * rstd_rows
    return (unit_rows * gain + shift, unit_rows, rstd_rows)


def norm_back(grad_norm, unit_rows, rstd_rows, gain):
    scaled = grad_norm * gain
    return rstd_rows * (
        scaled
        - jnp.mean(scaled, -1, keepdims=True)
        - unit_rows * jnp.mean(scaled * unit_rows, -1, keepdims=True)
    )


def gelu_exact(values):
    return jax.nn.gelu(values, approximate=False)


def local(
    inputs,
    cotangent,
    span_table,
    ln1_gain,
    ln1_shift,
    w_query,
    b_query,
    w_key,
    w_value,
    b_value,
    w_out,
    b_out,
    ln2_gain,
    ln2_shift,
    w_up,
    b_up,
    w_down,
    b_down,
):
    bfloat = jnp.bfloat16
    single = jnp.float32
    tok_rows = inputs.shape[0]
    seq_count = span_table.shape[0]
    seq_len = tok_rows // seq_count
    mp_size = lax.axis_size("mp")
    share_rows = tok_rows // mp_size
    first_row = lax.axis_index("mp") * share_rows
    head_count = w_query.shape[1] // HD

    def by_heads(matrix):
        return matrix.reshape(seq_count, seq_len, head_count, HD)

    def own_rows(matrix):
        return lax.dynamic_slice_in_dim(matrix, first_row, share_rows, 0)

    inputs_f = inputs.astype(single)
    gain_one = ln1_gain.astype(single)
    shift_one = ln1_shift.astype(single)
    gain_two = ln2_gain.astype(single)
    shift_two = ln2_shift.astype(single)
    bias_out = b_out.astype(single)
    bias_down = b_down.astype(single)
    norm_one, unit_one, rstd_one = normalize(inputs_f, gain_one, shift_one)
    normed_one = norm_one.astype(bfloat)
    query = (matmul(normed_one, w_query) + b_query.astype(single)).astype(bfloat)
    key_rows = matmul(normed_one, w_key).astype(bfloat)
    value_rows = (matmul(normed_one, w_value) + b_value.astype(single)).astype(bfloat)
    scores = (
        jnp.einsum(
            "sqhd,skhd->shqk", by_heads(query), by_heads(key_rows), preferred_element_type=single
        )
        * 0.125
    )
    row_max = jnp.max(scores, -1, keepdims=True)
    exp_terms = jnp.exp(scores - row_max)
    denom_sum = jnp.sum(exp_terms, -1, keepdims=True)
    log_total = row_max + jnp.log(denom_sum)
    prob_low = (exp_terms / denom_sum).astype(bfloat)
    mixed = jnp.einsum(
        "shqk,skhd->sqhd", prob_low, by_heads(value_rows), preferred_element_type=single
    )
    mixed = mixed.reshape(tok_rows, head_count * HD).astype(bfloat)
    branch = (
        lax.psum(matmul(mixed, w_out).astype(jnp.bfloat16), "mp").astype(jnp.float32) + bias_out
    )
    resid = inputs_f + branch
    norm_two, unit_two, rstd_two = normalize(resid, gain_two, shift_two)
    normed_two = norm_two.astype(bfloat)
    hidden_pre = matmul(normed_two, w_up) + b_up.astype(single)
    hidden, gelu_pull = jax.vjp(gelu_exact, hidden_pre)
    hidden_low = hidden.astype(bfloat)
    ffn_full = lax.psum(matmul(hidden_low, w_down).astype(jnp.bfloat16), "mp").astype(jnp.float32)
    layer_out = own_rows(resid + ffn_full + bias_down).astype(bfloat)
    positions = jnp.arange(seq_len, dtype=jnp.int32)[None, :]
    span_start = span_table[:, 0:1]
    span_len = span_table[:, 1:2]
    span_mask = ((positions >= span_start) & (positions < span_start + span_len)).astype(single)
    grad_out = cotangent.astype(single) * span_mask.reshape(tok_rows, 1)
    grad_low = grad_out.astype(bfloat)
    grad_w_down = matmul_tn(hidden_low, grad_low)
    grad_b_down_part = jnp.sum(own_rows(grad_out), 0)
    grad_hidden = matmul_nt(grad_low, w_down)
    grad_pre = gelu_pull(grad_hidden)[0].astype(bfloat)
    grad_w_up = matmul_tn(normed_two, grad_pre)
    grad_b_up = jnp.sum(grad_pre, 0, dtype=single)
    grad_norm_two = lax.psum(matmul_nt(grad_pre, w_up).astype(jnp.bfloat16), "mp").astype(
        jnp.float32
    )
    grad_resid = grad_out + norm_back(grad_norm_two, unit_two, rstd_two, gain_two)
    grad_branch = grad_resid.astype(bfloat)
    norm_two_part = own_rows(grad_norm_two)
    unit_two_part = own_rows(unit_two)
    resid_part = own_rows(grad_resid)
    grad_w_out = matmul_tn(mixed, grad_branch)
    grad_b_out_part = jnp.sum(own_rows(grad_branch), 0, dtype=single)
    grad_mixed = matmul_nt(grad_branch, w_out).astype(bfloat)
    scores_again = (
        jnp.einsum(
            "sqhd,skhd->shqk", by_heads(query), by_heads(key_rows), preferred_element_type=single
        )
        * 0.125
    )
    prob_again = jnp.exp(scores_again - log_total)
    prob_again_low = prob_again.astype(bfloat)
    grad_prob = jnp.einsum(
        "sqhd,skhd->shqk", by_heads(grad_mixed), by_heads(value_rows), preferred_element_type=single
    )
    row_dot = jnp.sum(prob_again * grad_prob, -1, keepdims=True)
    grad_scores = (prob_again * (grad_prob - row_dot)).astype(bfloat)
    grad_query = (
        jnp.einsum(
            "shqk,skhd->sqhd", grad_scores, by_heads(key_rows), preferred_element_type=single
        )
        * 0.125
    )
    grad_query = grad_query.reshape(tok_rows, head_count * HD).astype(bfloat)
    grad_key = (
        jnp.einsum("shqk,sqhd->skhd", grad_scores, by_heads(query), preferred_element_type=single)
        * 0.125
    )
    grad_key = grad_key.reshape(tok_rows, head_count * HD).astype(bfloat)
    grad_value = jnp.einsum(
        "shqk,sqhd->skhd", prob_again_low, by_heads(grad_mixed), preferred_element_type=single
    )
    grad_value = grad_value.reshape(tok_rows, head_count * HD).astype(bfloat)
    grad_w_query = matmul_tn(normed_one, grad_query)
    grad_b_query = jnp.sum(grad_query, 0, dtype=single)
    grad_w_key = matmul_tn(normed_one, grad_key)
    grad_w_value = matmul_tn(normed_one, grad_value)
    grad_b_value = jnp.sum(grad_value, 0, dtype=single)
    grad_norm_all = (
        matmul_nt(grad_query, w_query) + matmul_nt(grad_key, w_key) + matmul_nt(grad_value, w_value)
    )
    grad_norm_one = own_rows(lax.psum(grad_norm_all.astype(jnp.bfloat16), "mp").astype(jnp.float32))
    unit_one_part = own_rows(unit_one)
    grad_inputs = (
        resid_part + norm_back(grad_norm_one, unit_one_part, own_rows(rstd_one), gain_one)
    ).astype(bfloat)
    small_sums = lax.psum(
        (
            jnp.sum(grad_norm_one * unit_one_part, 0),
            jnp.sum(grad_norm_one, 0),
            jnp.sum(norm_two_part * unit_two_part, 0),
            jnp.sum(norm_two_part, 0),
            grad_b_out_part,
            grad_b_down_part,
        ),
        ("dp", "mp"),
    )
    grad_ln1_gain, grad_ln1_shift, grad_ln2_gain, grad_ln2_shift, grad_b_out, grad_b_down = (
        small_sums
    )
    (
        grad_w_query,
        grad_b_query,
        grad_w_key,
        grad_w_value,
        grad_b_value,
        grad_w_out,
        grad_w_up,
        grad_b_up,
        grad_w_down,
    ) = lax.psum(
        (
            grad_w_query,
            grad_b_query,
            grad_w_key,
            grad_w_value,
            grad_b_value,
            grad_w_out,
            grad_w_up,
            grad_b_up,
            grad_w_down,
        ),
        "dp",
    )
    return (
        layer_out,
        grad_inputs,
        grad_ln1_gain,
        grad_ln1_shift,
        grad_w_query,
        grad_b_query,
        grad_w_key,
        grad_w_value,
        grad_b_value,
        grad_w_out,
        grad_b_out,
        grad_ln2_gain,
        grad_ln2_shift,
        grad_w_up,
        grad_b_up,
        grad_w_down,
        grad_b_down,
    )


def solution(mesh):
    return jax.shard_map(
        local,
        mesh=mesh,
        in_specs=(
            P("dp", None),
            P("dp", None),
            P("dp", None),
            P(),
            P(),
            P(None, "mp"),
            P("mp"),
            P(None, "mp"),
            P(None, "mp"),
            P("mp"),
            P("mp", None),
            P(),
            P(),
            P(),
            P(None, "mp"),
            P("mp"),
            P("mp", None),
            P(),
        ),
        out_specs=(
            P(("dp", "mp"), None),
            P(("dp", "mp"), None),
            P(),
            P(),
            P(None, "mp"),
            P("mp"),
            P(None, "mp"),
            P(None, "mp"),
            P("mp"),
            P("mp", None),
            P(),
            P(),
            P(),
            P(None, "mp"),
            P("mp"),
            P("mp", None),
            P(),
        ),
        check_vma=False,
    )
```

profile of v0, /device:TPU:0, one launch (start us, length us, event | category | flops | bytes accessed | tf_op | source)
XLA Modules:
  0.0 738.2 jit_solution(5827203287279310220)
XLA Ops:
  10.3 2.4 convert_reduce_fusion
  12.7 2.9 fusion.4
  15.7 3.4 fusion.2
  22.5 3.1 fusion.16
  26.1 4.2 convolution_convert_fusion.4
  30.4 2.3 reshape.173
  36.7 2.4 copy-done.2
  39.3 3.2 fusion.40
  43.3 2.7 convolution_convert_fusion.2
  50.1 119.9 %all-reduce.9.cloned.1.call-done = bf16[2048,768]{1,0:T(8,128)(2,1)} async-done(((bf16[2048,768]{1,0:T(8,128)(2,1)}), bf16[2048,768]{1,0:T(8,128)(2,1)}) %all-reduce.9.cloned.1.call-update) | async-done | bytes 3145744 | tf_op jit(solution)/shard_map/psum | solution.py:112
  170.0 3.9 fusion.58
  176.7 16.9 %multiply_convert_fusion.1 = (bf16[2048,768]{1,0:T(8,128)(2,1)}, f32[2048,768]{1,0:T(8,128)S(1)}, f32[2048,768]{1,0:T(8,128)S(1)}) fusion(f32[768]{0:T(1024)S(1)} %copy-done.35, bf16[768,768]{1,0:T(8,128)(2,1)S(1)} %copy-done, f32[2048,768]{1,0:T(8,128)S(1)} %subtract_multiply_fusion, f32[768]{0:T(1024)S(1)} %convert_element_type.185, ...), kind=kOutput, calls=%fused_computation.24 | convolution fusion | flops 2524446720 | bytes 23208960 | tf_op jit(solution)/shard_map/dot_general | solution.py:13
  193.6 5.6 convert_reduce_fusion.1
  200.8 4.0 convolution_convert_fusion
  205.7 6.5 convolution_convert_fusion.1
  212.3 112.9 %all-reduce.11.cloned.1.call-done = bf16[2048,768]{1,0:T(8,128)(2,1)} async-done(((bf16[2048,768]{1,0:T(8,128)(2,1)}), bf16[2048,768]{1,0:T(8,128)(2,1)}) %all-reduce.11.cloned.1.call-update) | async-done | bytes 3145744 | tf_op jit(solution)/shard_map/psum | solution.py:134
  325.1 5.1 multiply_reduce_fusion.4
  330.7 8.7 %fusion.56 = (bf16[2048,768]{1,0:T(8,128)(2,1)S(1)}, f32[2048,768]{1,0:T(8,128)}, f32[2048,768]{1,0:T(8,128)}) fusion(f32[2048]{0:T(1024)S(1)} %broadcast_multiply_fusion, f32[2048]{0:T(1024)S(1)} %broadcast_multiply_fusion.1, f32[768]{0:T(1024)S(1)} %convert_element_type.184, bf16[2048,768]{1,0:T(8,128)(2,1)S(1)} %copy-done.8, f32[2048]{0:T(1024)S(1)} %copy-done.28, ...), kind=kLoop, calls=%fused_computation.114 | loop fusion | flops 18874368 | bytes 28355584 | tf_op jit(solution)/shard_map/convert_element_type | solution.py:138
  343.2 2.3 reshape.174
  345.5 7.2 convert_reduce_fusion.4
  352.7 9.1 %multiply_reduce_fusion = (f32[4,3,512]{2,1,0:T(4,128)S(1)}, f32[4,3,512,512]{2,3,1,0:T(8,128)}) fusion(f32[4,3,512,512]{2,3,1,0:T(8,128)} %copy-done.2, f32[4,3,512]{2,1,0:T(4,128)S(1)} %log_add_fusion, bf16[4,512,3,64]{1,0,3,2:T(4,128)(2,1)S(1)} %copy-done.12, bf16[4,512,3,64]{1,0,3,2:T(4,128)(2,1)S(1)} %reshape.174), kind=kOutput, calls=%fused_computation.1 | convolution fusion | flops 415229952 | bytes 26787840 | tf_op jit(solution)/shard_map/sqhd,skhd->shqk/dot_general | solution.py:153
  361.8 7.0 multiply_convert_fusion
  376.6 2.8 add_convert_fusion
  379.7 7.2 fusion.29
  386.9 7.1 fusion.41
  401.5 5.0 convert_element_type.199
  406.5 15.2 %all-reduce.1 = (f32[192]{0:T(256)}, f32[192]{0:T(256)}, f32[768]{0:T(1024)}) all-reduce(f32[192]{0:T(256)S(1)} %reduce_sum.188, f32[192]{0:T(256)S(1)} %reduce_sum.190, f32[768]{0:T(1024)S(1)} %copy-done.34), channel_id=1, replica_groups=mesh['dp'=8,'mp'=4] {'dp'}, use_global_device_ids=true, to_apply=%region_21.0 | all-reduce | flops 1152 | bytes 9216 | tf_op jit(solution)/shard_map/psum | solution.py:211
  425.6 176.2 %all-reduce.15.cloned.1.call-done = (bf16[2048,768]{1,0:T(8,128)(2,1)}, bf16[2048,768]{1,0:T(8,128)(2,1)}) async-done(((bf16[2048,768]{1,0:T(8,128)(2,1)}, bf16[2048,768]{1,0:T(8,128)(2,1)}), (bf16[2048,768]{1,0:T(8,128)(2,1)}, bf16[2048,768]{1,0:T(8,128)(2,1)})) %all-reduce.15.cloned.1.call-update) | async-done | bytes 6291472 | tf_op jit(solution)/shard_map/psum | solution.py:120
  601.8 2.2 fusion.26
  604.0 40.5 %all-reduce = (f32[768]{0:T(1024)}, f32[768]{0:T(1024)}, f32[768]{0:T(1024)}, f32[768]{0:T(1024)}, f32[768]{0:T(1024)}, /*index=5*/f32[768]{0:T(1024)}) all-reduce(f32[768]{0:T(1024)S(1)} %get-tuple-element.17, f32[768]{0:T(1024)S(1)} %get-tuple-element.24, ...), channel_id=1, replica_groups=mesh['dp'=8,'mp'=4] {'dp','mp'}, use_global_device_ids=true, to_apply=%region_16.0 | all-reduce | flops 4608 | bytes 36864 | tf_op jit(solution)/shard_map/psum | solution.py:187
  644.5 4.4 fusion.24
  648.9 71.6 %all-reduce.13.cloned.1.call-done = (f32[768,192]{0,1:T(8,128)}, f32[768,192]{0,1:T(8,128)}, f32[768,192]{0,1:T(8,128)}, f32[192,768]{1,0:T(8,128)}, f32[768,768]{1,0:T(8,128)}, /*index=5*/f32[768,768]{1,0:T(8,128)}) async-done(((f32[768,192]{0,1:T(8,128)}, f32[768,192]{0,1:T(8,128)}, f32[768,192]{0,1:T(8,128)}, f32[192,768]{1,0:T(8,128)}, f32[768,768]{1,0:T(8,128)}, /*index=5*/f32[768,768]{1,0:T(8,128)}), ...) | async-done | bytes 7077904 | tf_op jit(solution)/shard_map/psum | solution.py:211
  (150 shorter events, 55.5 us)
Async XLA Ops:
  7.2 169.4 %copy-start = (bf16[768,768]{1,0:T(8,128)(2,1)S(1)}, bf16[768,768]{1,0:T(8,128)(2,1)}, u32[]{:S(2)}) copy-start(bf16[768,768]{1,0:T(8,128)(2,1)} %param.32) | copy-start | bytes 3538948
  7.2 162.8 %all-reduce.9.cloned.1.call-start = ((), (), s32[]{:S(2)}) async-start(), calls=%async_computation | async-start | bytes 6291456 | tf_op jit(solution)/shard_map/psum | solution.py:112
  7.3 8.4 %copy-start.6 = (bf16[2048,768]{1,0:T(8,128)(2,1)S(1)}, bf16[2048,768]{1,0:T(8,128)(2,1)}, u32[]{:S(2)}) copy-start(bf16[2048,768]{1,0:T(8,128)(2,1)} %param.18) | copy-start | bytes 9437188
  9.6 9.4 %copy-start.29 = (f32[768]{0:T(1024)}, f32[768]{0:T(1024)S(1)}, u32[]{:S(2)}) copy-start(f32[768]{0:T(1024)S(1)} %convert_element_type.169) | copy-start | bytes 9220
  15.7 5.0 copy-start.20
  26.1 10.5 %copy-start.11 = (bf16[4,512,3,64]{1,0,3,2:T(4,128)(2,1)}, bf16[4,512,3,64]{1,0,3,2:T(4,128)(2,1)S(1)}, u32[]{:S(2)}) copy-start(bf16[4,512,3,64]{1,0,3,2:T(4,128)(2,1)S(1)} %reshape.171) | copy-start | bytes 2359300
  34.5 4.6 copy-start.2
  34.5 4.7 copy-start.19
  46.0 279.1 %all-reduce.11.cloned.1.call-start = ((), (), s32[]{:S(2)}) async-start(), calls=%async_computation.1 | async-start | bytes 6291456 | tf_op jit(solution)/shard_map/psum | solution.py:134
  176.6 16.9 %copy-start.7 = (f32[2048,768]{1,0:T(8,128)}, f32[2048,768]{1,0:T(8,128)S(1)}, u32[]{:S(2)}) copy-start(f32[2048,768]{1,0:T(8,128)S(1)} %subtract_multiply_fusion) | copy-start | bytes 18874372
  176.6 16.9 %copy-start.13 = (bf16[2048,768]{1,0:T(8,128)(2,1)S(1)}, bf16[2048,768]{1,0:T(8,128)(2,1)}, u32[]{:S(2)}) copy-start(bf16[2048,768]{1,0:T(8,128)(2,1)} %param.19) | copy-start | bytes 9437188
  176.7 16.9 %copy-start.32 = (f32[1,4,4,128]{3,1,2,0:T(4,128)S(1)}, f32[1,4,4,128]{3,1,2,0:T(4,128)}, u32[]{:S(2)}) copy-start(f32[1,4,4,128]{3,1,2,0:T(4,128)} %copy.68) | copy-start | bytes 24580
  176.7 16.9 %copy-start.39 = (bf16[768,768]{1,0:T(8,128)(2,1)S(1)}, bf16[768,768]{1,0:T(8,128)(2,1)}, u32[]{:S(2)}) copy-start(bf16[768,768]{1,0:T(8,128)(2,1)} %param.34) | copy-start | bytes 3538948
  204.9 396.9 %all-reduce.15.cloned.1.call-start = ((), (), s32[]{:S(2)}) async-start(), calls=%async_computation.3 | async-start | bytes 12582912 | tf_op jit(solution)/shard_map/psum | solution.py:120
  205.7 119.4 %copy-start.28 = (f32[2048]{0:T(1024)S(1)}, f32[2048]{0:T(1024)}, u32[]{:S(2)}) copy-start(f32[2048]{0:T(1024)} %copy-done.27) | copy-start | bytes 24580
  212.3 118.0 %copy-start.33 = (f32[1,4,4,128]{3,1,2,0:T(4,128)S(1)}, f32[1,4,4,128]{3,1,2,0:T(4,128)}, u32[]{:S(2)}) copy-start(f32[1,4,4,128]{3,1,2,0:T(4,128)} %copy.68) | copy-start | bytes 24580
  325.1 5.1 copy-start.8
  325.1 5.6 copy-start.14
  330.7 10.4 %copy-start.24 = (bf16[192,768]{1,0:T(8,128)(2,1)S(1)}, bf16[192,768]{1,0:T(8,128)(2,1)}, u32[]{:S(2)}) copy-start(bf16[192,768]{1,0:T(8,128)(2,1)} %param.28) | copy-start | bytes 884740
  345.4 7.2 copy-start.12
  345.5 16.3 %slice-start = ((s8[12582912]{0:T(1024)(128)(4,1)}), s8[4194304]{0:T(1024)(128)(4,1)S(1)}, s32[]{:S(2)}) async-start(s8[12582912]{0:T(1024)(128)(4,1)} %bitcast.75), calls=%async_computation.4 | async-start | bytes 8388608
  345.5 16.3 %slice-start.1 = ((s8[12582912]{0:T(1024)(128)(4,1)}), s8[4194304]{0:T(1024)(128)(4,1)S(1)}, s32[]{:S(2)}) async-start(s8[12582912]{0:T(1024)(128)(4,1)} %bitcast.75), calls=%async_computation.5 | async-start | bytes 8388608
  352.7 9.1 %slice-start.2 = ((s8[12582912]{0:T(1024)(128)(4,1)}), s8[4194304]{0:T(1024)(128)(4,1)S(1)}, s32[]{:S(2)}) async-start(s8[12582912]{0:T(1024)(128)(4,1)} %bitcast.75), calls=%async_computation.6 | async-start | bytes 8388608
  379.4 341.1 %all-reduce.13.cloned.1.call-start = ((), (), s32[]{:S(2)}) async-start(), calls=%async_computation.2 | async-start | bytes 14155776 | tf_op jit(solution)/shard_map/psum | solution.py:211
  379.7 7.2 copy-start.16
  386.9 7.1 copy-start.10
  386.9 8.7 %copy-start.5 = (bf16[2048,768]{1,0:T(8,128)(2,1)S(1)}, bf16[2048,768]{1,0:T(8,128)(2,1)}, u32[]{:S(2)}) copy-start(bf16[2048,768]{1,0:T(8,128)(2,1)} %copy-done.4) | copy-start | bytes 9437188
  400.5 6.0 copy-start.34
  401.5 200.3 %copy-start.30 = (f32[768]{0:T(1024)S(1)}, f32[768]{0:T(1024)}, u32[]{:S(2)}) copy-start(f32[768]{0:T(1024)} %copy-done.29) | copy-start | bytes 9220
  720.5 7.9 %copy-start.18 = (f32[768,768]{1,0:T(8,128)S(1)}, f32[768,768]{1,0:T(8,128)}, u32[]{:S(2)}) copy-start(f32[768,768]{1,0:T(8,128)} %get-tuple-element.81) | copy-start | bytes 7077892
  720.5 9.3 %copy-start.17 = (f32[768,768]{1,0:T(8,128)S(1)}, f32[768,768]{1,0:T(8,128)}, u32[]{:S(2)}) copy-start(f32[768,768]{1,0:T(8,128)} %get-tuple-element.83) | copy-start | bytes 7077892
  720.5 10.7 %copy-start.1 = (bf16[768,768]{1,0:T(8,128)(2,1)S(1)}, bf16[768,768]{1,0:T(8,128)(2,1)}, u32[]{:S(2)}) copy-start(bf16[768,768]{1,0:T(8,128)(2,1)} %param.32) | copy-start | bytes 3538948
  (15 other events, 34.2 us)
Sparse Core Ops, SparseCore 0:
  46.2 123.7 all-reduce.8
  205.0 120.0 all-reduce.10
  379.6 222.2 all-reduce.14
  606.9 113.5 all-reduce.12
where the time goes:
time: 747 us; the launch traced here: 738 us
  waiting for transfers between devices  481 us (64%)
  matrix products  96.5 us (13%)
  other arithmetic  59.8 us (8%)
  blocking collectives  55.7 us (7%)
  local copies, waits for them, and re-layouts  30.3 us (4%)
  between operations  14.8 us (2%)
    psum x1, waiting for transfers between devices, local(): lax.psum(matmul(hidden_low, w_down).astype(jnp.bfloat16), 'mp')  176 us
    psum x1, waiting for transfers between devices, local(): lax.psum(matmul(mixed, w_out).astype(jnp.bfloat16), 'mp')  120 us
    psum x1, waiting for transfers between devices, local(): lax.psum(matmul_nt(grad_pre, w_up).astype(jnp.bfloat16), 'mp')  113 us
    psum x1, waiting for transfers between devices, local(): lax.psum((grad_w_query, grad_b_query, grad_w_key, grad_w_value, grad_b_va...  71.6 us
    psum x1, blocking collectives, local(): lax.psum((jnp.sum(grad_norm_one * unit_one_part, 0), jnp.sum(grad_norm_on...  40.5 us
    dot_general x6, matrix products, matmul(): return jnp.dot(left, right, preferred_element_type=jnp.float32)  34.6 us
    unnamed x97, local copies, waits for them, and re-layouts  21.2 us
    dot_general x6, matrix products, matmul_tn(): lax.dot_general(left, right, (((0,), (0,)), ((), ())), preferred_element_...  20.7 us
  transfers between devices with their start and end apart: 4, of which 4 were waited for; matrix products, arithmetic and copies ran while one was open for 7% of the time, Pallas kernels for 0%

commit v1 on v0

v1 whole, which is shorter than its diff:
```python
import functools

import jax
import jax.numpy as jnp
from jax import lax
from jax.experimental import pallas as pl
from jax.experimental.pallas import tpu as pltpu
from jax.sharding import PartitionSpec as P

HD = 64
WIN = 128
EPS = 1e-06
SMALL = 16
MIB = 1 << 20

bf16 = jnp.bfloat16
f32 = jnp.float32


def mm(left, right):
    return lax.dot_general(left, right, (((1,), (0,)), ((), ())), preferred_element_type=f32)


def mm_nt(left, right):
    return lax.dot_general(left, right, (((1,), (1,)), ((), ())), preferred_element_type=f32)


def mm_tn(left, right):
    return lax.dot_general(left, right, (((0,), (0,)), ((), ())), preferred_element_type=f32)


def unit_of(values):
    centered = values - jnp.mean(values, -1, keepdims=True)
    rstd = lax.rsqrt(jnp.mean(centered * centered, -1, keepdims=True) + EPS)
    return centered * rstd, rstd


def norm_back(grad_norm, unit, rstd, gain):
    scaled = grad_norm * gain
    return rstd * (
        scaled
        - jnp.mean(scaled, -1, keepdims=True)
        - unit * jnp.mean(scaled * unit, -1, keepdims=True)
    )


def window_of(span_ref, seq, length):
    start = span_ref[seq, 0]
    count = span_ref[seq, 1]
    first = jnp.minimum(start, length - WIN)
    row = lax.broadcasted_iota(jnp.int32, (WIN, length), 0) + first
    col = lax.broadcasted_iota(jnp.int32, (WIN, length), 1)
    pick = row == col
    inside = pick & (row >= start) & (row < start + count)
    return pick.astype(f32).astype(bf16), inside.astype(f32).astype(bf16)


def softmax_parts(query, keys):
    scores = mm_nt(query, keys) * 0.125
    terms = jnp.exp(scores - jnp.max(scores, -1, keepdims=True))
    return terms, 1.0 / jnp.sum(terms, -1, keepdims=True)


def attend(query, keys, values):
    heads = []
    for h in range(keys.shape[1] // HD):
        cols = slice(h * HD, (h + 1) * HD)
        terms, inverse = softmax_parts(query[:, cols], keys[:, cols])
        heads.append(mm(terms.astype(bf16), values[:, cols]) * inverse)
    return jnp.concatenate(heads, 1).astype(bf16)


def attend_back(query, keys, values, grad_mixed):
    grad_q, grad_k, grad_v = [], [], []
    for h in range(keys.shape[1] // HD):
        cols = slice(h * HD, (h + 1) * HD)
        q, k, v, g = query[:, cols], keys[:, cols], values[:, cols], grad_mixed[:, cols]
        terms, inverse = softmax_parts(q, k)
        prob = terms * inverse
        grad_prob = mm_nt(g, v)
        row_dot = jnp.sum(prob * grad_prob, -1, keepdims=True)
        grad_scores = (prob * (grad_prob - row_dot)).astype(bf16)
        grad_q.append(mm(grad_scores, k) * 0.125)
        grad_k.append(mm_tn(grad_scores, q) * 0.125)
        grad_v.append(mm_tn(prob.astype(bf16), g))
    return tuple(jnp.concatenate(part, 1).astype(bf16) for part in (grad_q, grad_k, grad_v))


def gelu_parts(values):
    phi = 0.5 * (1.0 + lax.erf(values * 0.7071067811865476))
    return phi


def first_kernel(
    span_ref, x_ref, cot_ref, gain_ref, shift_ref, wq_ref, wk_ref, wv_ref, bq_ref, bv_ref,
    normed_ref, xw_ref, gw_ref, nw_ref, qw_ref, k_ref, v_ref, mw_ref,
):
    length = x_ref.shape[0]
    x = x_ref[...]
    unit, _ = unit_of(x.astype(f32))
    normed = (unit * gain_ref[...].astype(f32) + shift_ref[...].astype(f32)).astype(bf16)
    normed_ref[...] = normed
    pick, inside = window_of(span_ref, pl.program_id(0), length)
    xw_ref[...] = mm(pick, x).astype(bf16)
    gw_ref[...] = mm(inside, cot_ref[...]).astype(bf16)
    nw = mm(pick, normed).astype(bf16)
    nw_ref[...] = nw
    query = (mm(nw, wq_ref[...]) + bq_ref[...].astype(f32)).astype(bf16)
    keys = mm(normed, wk_ref[...]).astype(bf16)
    values = (mm(normed, wv_ref[...]) + bv_ref[...].astype(f32)).astype(bf16)
    qw_ref[...] = query
    k_ref[...] = keys
    v_ref[...] = values
    mw_ref[...] = attend(query, keys, values)


def ffn_kernel(
    ids_ref, m0_ref, m1_ref, m2_ref, m3_ref, wo0_ref, wo_mine_ref, wo_other_ref, xw_ref, gw_ref,
    bout_ref, gain_ref, shift_ref, wup_ref, bup_ref, wdown_ref,
    keep_ref, send_ref, p0_ref, p1_ref, p2_ref, p3_ref, resid_ref, gown_ref, small_ref,
    wo_s, resid_s, part_s,
):
    own, core, parts = ids_ref[0], ids_ref[1], ids_ref[3]
    half = wo_mine_ref.shape[1]
    for i in range(3):
        wo_s[i, pl.ds(pl.multiple_of(core * half, 16), half), :] = wo_mine_ref[i]
        wo_s[i, pl.ds(pl.multiple_of((1 - core) * half, 16), half), :] = wo_other_ref[i]
    branch = mm(m0_ref[...], wo0_ref[...])
    for i, m_ref in enumerate((m1_ref, m2_ref, m3_ref)):
        branch += mm(m_ref[...], wo_s[i])
    resid = xw_ref[...].astype(f32) + (branch + bout_ref[...].astype(f32))
    resid_s[...] = resid
    unit, _ = unit_of(resid)
    normed = (unit * gain_ref[...].astype(f32) + shift_ref[...].astype(f32)).astype(bf16)
    pre = mm(normed, wup_ref[...]) + bup_ref[...].astype(f32)
    phi = gelu_parts(pre)
    hidden = (pre * phi).astype(bf16)
    slope = phi + pre * (0.3989422804014327 * jnp.exp(-0.5 * pre * pre))
    grad_out = gw_ref[...]
    grad_pre = (slope * mm_nt(grad_out, wdown_ref[...])).astype(bf16)
    grad_up = mm_tn(normed, grad_pre).astype(bf16)
    grad_down = mm_tn(hidden, grad_out).astype(bf16)

    @pl.when(core == 0)
    def _():
        keep_ref[...] = grad_up
        send_ref[...] = grad_down

    @pl.when(core == 1)
    def _():
        keep_ref[...] = grad_down
        send_ref[...] = grad_up

    part_s[...] = mm_nt(grad_pre, wup_ref[...])
    for r, p_ref in enumerate((p0_ref, p1_ref, p2_ref, p3_ref)):
        rows = pl.ds(pl.multiple_of(lax.rem(own + r, parts) * WIN, WIN), WIN)
        p_ref[...] = part_s[rows, :].astype(bf16)
    rows = pl.ds(pl.multiple_of(own * WIN, WIN), WIN)
    resid_ref[...] = resid_s[rows, :]
    gown_ref[...] = gw_ref[rows, :]
    small_ref[...] = jnp.zeros_like(small_ref)
    small_ref[0:1, :] = jnp.sum(grad_pre.astype(f32), 0, keepdims=True)
    small_ref[1:2, :] = jnp.sum(grad_out.astype(f32), 0, keepdims=True)


def norm_two_kernel(p0_ref, p1_ref, p2_ref, p3_ref, resid_ref, gown_ref, gain_ref, gresid_ref, gb_ref):
    grad_norm = p0_ref[...].astype(f32)
    for p_ref in (p1_ref, p2_ref, p3_ref):
        grad_norm += p_ref[...].astype(f32)
    unit, rstd = unit_of(resid_ref[...])
    grad = gown_ref[...].astype(f32) + norm_back(grad_norm, unit, rstd, gain_ref[...].astype(f32))
    gresid_ref[...] = grad
    gb_ref[0:WIN, :] = grad.astype(bf16)
    sums = [jnp.sum(grad_norm * unit, 0, keepdims=True), jnp.sum(grad_norm, 0, keepdims=True)]
    sums.append(jnp.zeros((SMALL - 2, grad.shape[1]), f32))
    gb_ref[WIN : WIN + SMALL, :] = jnp.concatenate(sums, 0).astype(bf16)


def attn_kernel(
    ids_ref, g0_ref, g1_ref, g2_ref, g3_ref, mw_ref, nw_ref, qw_ref, k_ref, v_ref, normed_ref,
    wq_ref, wk_ref, wv_ref, wo_ref, gain_ref, shift_ref, ffn_small_ref,
    keep_ref, send_ref, gb_s, acc_s, col_s,
):
    step = pl.program_id(0)
    width = wq_ref.shape[1]

    @pl.when(step == 0)
    def _():
        for i, g_ref in enumerate((g0_ref, g1_ref, g2_ref, g3_ref)):
            gb_s[i] = g_ref[...]
        acc_s[...] = jnp.zeros_like(acc_s)
        col_s[...] = jnp.zeros_like(col_s)

    block = gb_s[step]
    grad_branch = block[0:WIN]
    grad_mixed = mm_nt(grad_branch, wo_ref[...]).astype(bf16)
    grad_q, grad_k, grad_v = attend_back(qw_ref[...], k_ref[...], v_ref[...], grad_mixed)
    normed = normed_ref[...]
    acc_s[0] += mm_tn(grad_q, nw_ref[...])
    acc_s[1] += mm_tn(grad_k, normed)
    acc_s[2] += mm_tn(grad_v, normed)
    acc_s[3] += mm_tn(mw_ref[...], grad_branch)
    for i, grad in enumerate((grad_q, grad_k, grad_v)):
        col_s[i : i + 1, 0:width] += jnp.sum(grad.astype(f32), 0, keepdims=True)
    col_s[3:4, :] += jnp.sum(grad_branch.astype(f32), 0, keepdims=True)
    col_s[4:6, :] += block[WIN : WIN + 2].astype(f32)

    @pl.when(step == pl.num_programs(0) - 1)
    def _():
        core = ids_ref[1]
        eye = (
            lax.broadcasted_iota(jnp.int32, (width, width), 0)
            == lax.broadcasted_iota(jnp.int32, (width, width), 1)
        )
        eye = eye.astype(f32).astype(bf16)
        sums = jnp.zeros((1, gb_s.shape[2]), f32)
        cols = jnp.zeros((1, gb_s.shape[2]), f32)
        for i, w_ref in enumerate((wq_ref, wk_ref, wv_ref)):
            turned = mm_nt(eye, w_ref[...])
            sums += jnp.sum(turned * acc_s[i], 0, keepdims=True)
            total = col_s[i : i + 1, 0:width]
            high = total.astype(bf16)
            low = (total - high.astype(f32)).astype(bf16)
            both = jnp.concatenate([high, low, jnp.zeros((14, width), bf16)], 0)
            cols += jnp.sum(mm_nt(both, w_ref[...]), 0, keepdims=True)
        gain = (sums - shift_ref[...].astype(f32) * cols) / gain_ref[...].astype(f32)
        small = jnp.concatenate(
            [ffn_small_ref[0:2, :], col_s[3:6, :], gain, cols, col_s[0:1, :], col_s[2:3, :],
             jnp.zeros((SMALL - 9, gb_s.shape[2]), f32)], 0
        ).astype(bf16)
        first = jnp.concatenate([acc_s[0], acc_s[1]], 0).astype(bf16)
        second = jnp.concatenate([acc_s[2], acc_s[3]], 0).astype(bf16)
        rows = first.shape[0]
        keep_ref[rows : rows + SMALL, :] = small
        send_ref[rows : rows + SMALL, :] = small

        @pl.when(core == 0)
        def _():
            keep_ref[0:rows, :] = first
            send_ref[0:rows, :] = second

        @pl.when(core == 1)
        def _():
            keep_ref[0:rows, :] = second
            send_ref[0:rows, :] = first


def split_kernel(small, ids_ref, keep_ref, recv_ref, own_ref, *out_refs):
    chip = ids_ref[2]
    rows = (keep_ref.shape[0] - small) // 4
    outs = (own_ref,) + out_refs
    for flip, out_ref in enumerate(outs):
        part = pl.ds(pl.multiple_of((chip ^ flip) * rows, 16), rows)
        total = keep_ref[part, :].astype(f32) + recv_ref[part, :].astype(f32)
        out_ref[0:rows, :] = total.astype(out_ref.dtype)
    if small:
        part = slice(4 * rows, 4 * rows + small)
        total = keep_ref[part, :].astype(f32) + recv_ref[part, :].astype(f32)
        for out_ref in outs:
            out_ref[rows : rows + small, :] = total.astype(out_ref.dtype)


def total_kernel(own_ref, a_ref, b_ref, c_ref, out_ref, *small_refs):
    total = own_ref[...]
    for ref in (a_ref, b_ref, c_ref):
        total += ref[...].astype(f32)
    rows = out_ref.shape[0]
    out_ref[...] = total[0:rows].astype(bf16)
    if small_refs:
        small_refs[0][...] = total[rows:]


def place_kernel(ids_ref, *refs):
    chip = ids_ref[2]
    out_ref = refs[-1]
    rows = refs[0].shape[0]
    for flip, ref in enumerate(refs[:-1]):
        out_ref[pl.ds(pl.multiple_of((chip ^ flip) * rows, 16), rows), :] = ref[...]


def ffn_out_kernel(ids_ref, mine_ref, other_ref, up_ref, down_ref):
    core = ids_ref[1]

    @pl.when(core == 0)
    def _():
        up_ref[...] = mine_ref[...].astype(f32)
        down_ref[...] = other_ref[...].astype(f32)

    @pl.when(core == 1)
    def _():
        up_ref[...] = other_ref[...].astype(f32)
        down_ref[...] = mine_ref[...].astype(f32)


def attn_out_kernel(ids_ref, mine_ref, other_ref, q_ref, k_ref, v_ref, o_ref):
    core = ids_ref[1]
    width = o_ref.shape[0]

    def write(first_ref, second_ref):
        q_ref[...] = first_ref[0:width, :].astype(f32).T
        k_ref[...] = first_ref[width : 2 * width, :].astype(f32).T
        v_ref[...] = second_ref[0:width, :].astype(f32).T
        o_ref[...] = second_ref[width : 2 * width, :].astype(f32)

    pl.when(core == 0)(lambda: write(mine_ref, other_ref))
    pl.when(core == 1)(lambda: write(other_ref, mine_ref))


def load_pieces(pieces, arrays, ids_ref, first_col, buffer, sems, rel, start):
    width = buffer.shape[-1]
    number = 0
    for array, row, source, part, flip_bit, flip_core in pieces:
        if source != rel:
            continue
        rows = 96
        bit = ids_ref[4 + part] ^ flip_bit
        core = ids_ref[1] ^ flip_core
        place = pl.multiple_of(part * (4 * rows) + (bit * 2 + core) * rows, 16)
        copy = pltpu.make_async_copy(
            arrays[array].at[pl.ds(row, rows), pl.ds(first_col, width)],
            buffer.at[rel, pl.ds(place, rows), :],
            sems.at[rel, number],
        )
        number += 1
        if start:
            copy.start()
        else:
            copy.wait()


def load_bias(arrays, where, first_col, buffer, sems, rel, start):
    array, row = where[rel]
    copy = pltpu.make_async_copy(
        arrays[array].at[pl.ds(row, SMALL), pl.ds(first_col, buffer.shape[-1])],
        buffer.at[rel],
        sems.at[rel],
    )
    if start:
        copy.start()
    else:
        copy.wait()


def local_attn_kernel(
    layout, ids_ref, x_ref, normed_ref, wqkv_ref, wo0_ref, wo_mine_ref, wo_other_ref, bout_ref,
    gain_ref, shift_ref, *refs,
):
    arrays = refs[: layout.count]
    qkv_ref, wo_ref, resid_ref, normed_two_ref = refs[layout.count : layout.count + 4]
    w_s, b_s, acc_s, w_sem, b_sem, own_sem = refs[layout.count + 4 :]
    step = pl.program_id(0)
    width = wo0_ref.shape[0]
    half = wo_mine_ref.shape[1]
    own_copy = pltpu.make_async_copy(wqkv_ref, w_s.at[0], own_sem)

    @pl.when(step == 0)
    def _():
        own_copy.start()
        for rel in range(4):
            load_bias(arrays, layout.bias, layout.qkv_col, b_s, b_sem, rel, True)
        for rel in range(1, 4):
            load_pieces(layout.pieces, arrays, ids_ref, layout.qkv_col, w_s, w_sem, rel, True)
        acc_s[...] = x_ref[...].astype(f32) + bout_ref[...].astype(f32)
        own_copy.wait()
        wo_ref[...] = wo0_ref[...]

    for rel in range(1, 4):

        @pl.when(step == rel)
        def _(rel=rel):
            load_pieces(layout.pieces, arrays, ids_ref, layout.qkv_col, w_s, w_sem, rel, False)
            core = ids_ref[1]
            wo_ref[pl.ds(pl.multiple_of(core * half, 16), half), :] = wo_mine_ref[rel - 1]
            wo_ref[pl.ds(pl.multiple_of((1 - core) * half, 16), half), :] = wo_other_ref[rel - 1]

    for rel in range(4):

        @pl.when(step == rel)
        def _(rel=rel):
            load_bias(arrays, layout.bias, layout.qkv_col, b_s, b_sem, rel, False)

    qkv = (mm(normed_ref[...], w_s[step]) + b_s[step][0:1, :].astype(f32)).astype(bf16)
    qkv_ref[...] = qkv
    mixed = attend(qkv[:, 0:width], qkv[:, width : 2 * width], qkv[:, 2 * width : 3 * width])
    acc_s[...] += mm(mixed, wo_ref[...])

    @pl.when(step == 3)
    def _():
        resid = acc_s[...]
        resid_ref[...] = resid
        unit, _ = unit_of(resid)
        normed_two_ref[...] = (
            unit * gain_ref[...].astype(f32) + shift_ref[...].astype(f32)
        ).astype(bf16)


def local_ffn_kernel(
    layout, ids_ref, resid_ref, normed_ref, wup_ref, wdown_ref, bdown_ref, *refs
):
    arrays = refs[: layout.count]
    out_ref = refs[layout.count]
    up_s, down_s, b_s, acc_s, up_sem, down_sem, b_sem, own_sem = refs[layout.count + 1 :]
    step = pl.program_id(0)
    own_up = pltpu.make_async_copy(wup_ref, up_s.at[0], own_sem.at[0])
    own_down = pltpu.make_async_copy(wdown_ref, down_s.at[0], own_sem.at[1])

    @pl.when(step == 0)
    def _():
        own_up.start()
        for rel in range(4):
            load_bias(arrays, layout.bias, layout.up_col, b_s, b_sem, rel, True)
        own_down.start()
        for rel in range(1, 4):
            load_pieces(layout.pieces, arrays, ids_ref, layout.up_col, up_s, up_sem, rel, True)
            load_pieces(layout.pieces, arrays, ids_ref, layout.down_col, down_s, down_sem, rel, True)
        acc_s[...] = resid_ref[...] + bdown_ref[...].astype(f32)
        own_up.wait()
        own_down.wait()

    for rel in range(4):

        @pl.when(step == rel)
        def _(rel=rel):
            load_bias(arrays, layout.bias, layout.up_col, b_s, b_sem, rel, False)
            if rel:
                load_pieces(layout.pieces, arrays, ids_ref, layout.up_col, up_s, up_sem, rel, False)
                load_pieces(
                    layout.pieces, arrays, ids_ref, layout.down_col, down_s, down_sem, rel, False
                )

    pre = mm(normed_ref[...], up_s[step]) + b_s[step][0:1, :].astype(f32)
    hidden = (pre * gelu_parts(pre)).astype(bf16)
    acc_s[...] += mm(hidden, down_s[step])

    @pl.when(step == 3)
    def _():
        out_ref[...] = acc_s[...].astype(bf16)


def local_back_kernel(
    layout, span_ref, ids_ref, x_ref, gresid_ref, gb_ref, qkv_ref, wo_ref, wqkv_ref, gain_ref, *refs
):
    arrays = refs[: layout.count]
    out_ref = refs[layout.count]
    w_s, acc_s, w_sem, own_sem = refs[layout.count + 1 :]
    step = pl.program_id(0)
    length = x_ref.shape[0]
    width = wo_ref.shape[0]
    own_copy = pltpu.make_async_copy(wqkv_ref, w_s.at[0], own_sem)

    @pl.when(step == 0)
    def _():
        own_copy.start()
        for rel in range(1, 4):
            load_pieces(layout.pieces, arrays, ids_ref, layout.qkv_col, w_s, w_sem, rel, True)
        acc_s[...] = jnp.zeros_like(acc_s)
        own_copy.wait()

    for rel in range(1, 4):

        @pl.when(step == rel)
        def _(rel=rel):
            load_pieces(layout.pieces, arrays, ids_ref, layout.qkv_col, w_s, w_sem, rel, False)

    pick, _ = window_of(span_ref, ids_ref[0], length)
    qkv = qkv_ref[...]
    query = mm(pick, qkv[:, 0:width]).astype(bf16)
    grad_mixed = mm_nt(gb_ref[0:WIN, :], wo_ref[...]).astype(bf16)
    grad_q, grad_k, grad_v = attend_back(
        query, qkv[:, width : 2 * width], qkv[:, 2 * width : 3 * width], grad_mixed
    )
    grad_q = mm_tn(pick, grad_q).astype(bf16)
    grads = jnp.concatenate(
        [grad_q, grad_k, grad_v, jnp.zeros((length, w_s.shape[2] - 3 * width), bf16)], 1
    )
    acc_s[...] += mm_nt(grads, w_s[step])

    @pl.when(step == 3)
    def _():
        unit, rstd = unit_of(x_ref[...].astype(f32))
        grad = norm_back(acc_s[...], unit, rstd, gain_ref[...].astype(f32))
        resid = gresid_ref[...]
        high = resid.astype(bf16)
        low = (resid - high.astype(f32)).astype(bf16)
        out_ref[...] = (grad + mm_tn(pick, high) + mm_tn(pick, low)).astype(bf16)


class Layout:
    def __init__(self, count, pieces, bias, up_col, qkv_col, down_col):
        self.count = count
        self.pieces = pieces
        self.bias = bias
        self.up_col = up_col
        self.qkv_col = qkv_col
        self.down_col = down_col


def sds(shape, dtype):
    return jax.ShapeDtypeStruct(shape, dtype)


def params(mib=48):
    return pltpu.CompilerParams(vmem_limit_bytes=mib * MIB)


SMEM = pl.BlockSpec(memory_space=pltpu.SMEM)
VMEM = pl.BlockSpec(memory_space=pltpu.VMEM)
ANY = pl.BlockSpec(memory_space=pl.ANY)


def local(
    dp_size, mp_size, inputs, cotangent, span_table, ln1_gain, ln1_shift, w_query, b_query, w_key,
    w_value, b_value, w_out, b_out, ln2_gain, ln2_shift, w_up, b_up, w_down, b_down,
):
    tok_rows, model = inputs.shape
    seqs = span_table.shape[0]
    length = tok_rows // seqs
    width = w_query.shape[1]
    units = w_up.shape[1]
    dp_bits = dp_size.bit_length() - 1
    bit_x, bit_y = 1, dp_bits - 1
    dp_idx = lax.axis_index("dp")
    own = lax.axis_index("mp")
    core = dp_idx & 1
    at_x = (dp_idx >> bit_x) & 1
    at_y = (dp_idx >> bit_y) & 1
    ids = jnp.stack([own, core, at_y * 2 + at_x, jnp.int32(mp_size), at_x, at_y]).astype(jnp.int32)

    def from_rel(value, rel):
        return lax.ppermute(value, "mp", [(i, (i - rel) % mp_size) for i in range(mp_size)])

    def to_rel(value, rel):
        return from_rel(value, -rel)

    def swap(value, bits):
        return lax.ppermute(value, "dp", [(i, i ^ bits) for i in range(dp_size)])

    core_bit, x_bit, y_bit = 1, 1 << bit_x, 1 << bit_y

    def row(vector):
        return vector.reshape(1, -1)

    gain_one, shift_one = row(ln1_gain), row(ln1_shift)
    gain_two, shift_two = row(ln2_gain), row(ln2_shift)

    half = width // 2
    wo_half = lax.dynamic_slice_in_dim(w_out, core * half, half, 0)
    wo_mine = jnp.stack([from_rel(wo_half, rel) for rel in (1, 2, 3)])
    wo_other = swap(wo_mine, core_bit)

    def seq_rows(rows, cols):
        return pl.BlockSpec((rows, cols), lambda i, *_: (i, 0))

    def whole(array):
        return pl.BlockSpec(array.shape, lambda i, *_: (0,) * array.ndim)

    bq, bv = row(b_query), row(b_value)
    normed, xw, gw, nw, qw, keys, values, mw = pl.pallas_call(
        first_kernel,
        grid_spec=pltpu.PrefetchScalarGridSpec(
            num_scalar_prefetch=1,
            grid=(seqs,),
            in_specs=[seq_rows(length, model), seq_rows(length, model)]
            + [whole(a) for a in (gain_one, shift_one, w_query, w_key, w_value, bq, bv)],
            out_specs=[
                seq_rows(length, model),
                seq_rows(WIN, model),
                seq_rows(WIN, model),
                seq_rows(WIN, model),
                seq_rows(WIN, width),
                seq_rows(length, width),
                seq_rows(length, width),
                seq_rows(WIN, width),
            ],
        ),
        out_shape=[
            sds((tok_rows, model), bf16),
            sds((seqs * WIN, model), bf16),
            sds((seqs * WIN, model), bf16),
            sds((seqs * WIN, model), bf16),
            sds((seqs * WIN, width), bf16),
            sds((tok_rows, width), bf16),
            sds((tok_rows, width), bf16),
            sds((seqs * WIN, width), bf16),
        ],
        compiler_params=params(),
        name="windows_forward",
    )(span_table, inputs, cotangent, gain_one, shift_one, w_query, w_key, w_value, bq, bv)

    mixed_parts = [mw] + [from_rel(mw, rel) for rel in (1, 2, 3)]

    win_rows = seqs * WIN
    keep, send, p0, p1, p2, p3, resid_own, gown, ffn_small = pl.pallas_call(
        ffn_kernel,
        in_specs=[SMEM] + [VMEM] * 15,
        out_specs=[VMEM] * 9,
        out_shape=[sds((model, units), bf16)] * 2
        + [sds((WIN, model), bf16)] * 4
        + [sds((WIN, model), f32), sds((WIN, model), bf16), sds((8, model), f32)],
        scratch_shapes=[
            pltpu.VMEM((3, width, model), bf16),
            pltpu.VMEM((win_rows, model), f32),
            pltpu.VMEM((win_rows, model), f32),
        ],
        compiler_params=params(),
        name="windows_ffn",
    )(ids, *mixed_parts, w_out, wo_mine, wo_other, xw, gw, row(b_out), gain_two, shift_two, w_up,
      row(b_up), w_down)

    def sum_start(keep, send, small, name):
        recv = swap(send, core_bit)
        rows = (keep.shape[0] - small) // 4 + small
        return pl.pallas_call(
            functools.partial(split_kernel, small),
            in_specs=[SMEM, VMEM, VMEM],
            out_specs=[VMEM] * 4,
            out_shape=[sds((rows, model), f32)] + [sds((rows, model), bf16)] * 3,
            compiler_params=params(),
            name=name + "_split",
        )(ids, keep, recv)

    def sum_middle(parts, small, name):
        own_part, to_x, to_y, to_xy = parts
        rows = own_part.shape[0] - small
        outs = [sds((rows, model), bf16)] + ([sds((small, model), f32)] if small else [])
        got = (swap(to_x, x_bit), swap(to_y, y_bit), swap(to_xy, x_bit | y_bit))
        result = pl.pallas_call(
            total_kernel,
            in_specs=[VMEM] * 4,
            out_specs=[VMEM] * len(outs),
            out_shape=outs,
            compiler_params=params(),
            name=name + "_total",
        )(own_part, *got)
        done = result[0]
        rest = result[1] if small else None
        for bit in range(2, dp_bits - 1):
            done = (done.astype(f32) + swap(done, 1 << bit).astype(f32)).astype(bf16)
            if small:
                rest = rest + swap(rest, 1 << bit)
        return done, rest

    def sum_end(done, name):
        parts = (done, swap(done, x_bit), swap(done, y_bit), swap(done, x_bit | y_bit))
        mine = pl.pallas_call(
            place_kernel,
            in_specs=[SMEM] + [VMEM] * 4,
            out_specs=VMEM,
            out_shape=sds((4 * done.shape[0], model), bf16),
            compiler_params=params(),
            name=name + "_place",
        )(ids, *parts)
        return mine, swap(mine, core_bit)

    ffn_done, _ = sum_middle(sum_start(keep, send, 0, "ffn"), 0, "ffn")
    ffn_mine, ffn_other = sum_end(ffn_done, "ffn")
    grad_w_up, grad_w_down = pl.pallas_call(
        ffn_out_kernel,
        in_specs=[SMEM, VMEM, VMEM],
        out_specs=[VMEM] * 2,
        out_shape=[sds((model, units), f32), sds((units, model), f32)],
        compiler_params=params(),
        name="ffn_gradients",
    )(ids, ffn_mine, ffn_other)

    got = [to_rel(p, rel) for p, rel in ((p1, 1), (p2, 2), (p3, 3))]
    gresid, gb = pl.pallas_call(
        norm_two_kernel,
        in_specs=[VMEM] * 7,
        out_specs=[VMEM] * 2,
        out_shape=[sds((WIN, model), f32), sds((WIN + SMALL, model), bf16)],
        compiler_params=params(),
        name="windows_norm_back",
    )(p0, *got, resid_own, gown, gain_two)
    gb_parts = [gb] + [from_rel(gb, rel) for rel in (1, 2, 3)]

    def rel_rows(rows, cols):
        return pl.BlockSpec((rows, cols), lambda i, ids: (lax.rem(ids[0] + i, ids[3]), 0))

    att_rows = 2 * width + SMALL
    keep, send = pl.pallas_call(
        attn_kernel,
        grid_spec=pltpu.PrefetchScalarGridSpec(
            num_scalar_prefetch=1,
            grid=(seqs,),
            in_specs=[whole(g) for g in gb_parts]
            + [
                rel_rows(WIN, width),
                rel_rows(WIN, model),
                rel_rows(WIN, width),
                rel_rows(length, width),
                rel_rows(length, width),
                rel_rows(length, model),
            ]
            + [whole(a) for a in (w_query, w_key, w_value, w_out, gain_one, shift_one, ffn_small)],
            out_specs=[pl.BlockSpec((att_rows, model), lambda i, *_: (0, 0))] * 2,
            scratch_shapes=[
                pltpu.VMEM((seqs, WIN + SMALL, model), bf16),
                pltpu.VMEM((4, width, model), f32),
                pltpu.VMEM((8, model), f32),
            ],
        ),
        out_shape=[sds((att_rows, model), bf16)] * 2,
        compiler_params=params(),
        name="windows_attention_back",
    )(ids, *gb_parts, mw, nw, qw, keys, values, normed, w_query, w_key, w_value, w_out, gain_one,
      shift_one, ffn_small)

    att_done, small = sum_middle(sum_start(keep, send, SMALL, "att"), SMALL, "att")
    norm_rows = small[5:7]
    norm_sums = norm_rows + sum(from_rel(norm_rows, rel) for rel in (1, 2, 3))
    att_mine, att_other = sum_end(att_done, "att")
    grad_w_query, grad_w_key, grad_w_value, grad_w_out = pl.pallas_call(
        attn_out_kernel,
        in_specs=[SMEM, VMEM, VMEM],
        out_specs=[VMEM] * 4,
        out_shape=[sds((model, width), f32)] * 3 + [sds((width, model), f32)],
        compiler_params=params(),
        name="attention_gradients",
    )(ids, att_mine, att_other)

    qkv_cols = -(-3 * width // 128) * 128
    pad = qkv_cols - 3 * width
    wqkv = jnp.concatenate([w_query, w_key, w_value, jnp.zeros((model, pad), bf16)], 1)
    piece = model // 8

    def packed(first):
        return jnp.concatenate(
            [lax.dynamic_slice_in_dim(w, first, piece, 0) for w in (w_up, wqkv, w_down)], 1
        )

    bias_row = jnp.concatenate(
        [b_up, b_query, jnp.zeros((width,), bf16), b_value, jnp.zeros((pad + model,), bf16)]
    )
    bias_own = jnp.concatenate(
        [row(bias_row), jnp.zeros((SMALL - 1, bias_row.shape[0]), bf16)], 0
    )
    piece_p = packed((at_x * 2 + core) * piece)
    piece_q = packed(4 * piece + (at_y * 2 + core) * piece)
    message = jnp.concatenate([piece_p, bias_own, piece_q], 0)
    got3 = from_rel(message, 3)
    got1 = from_rel(message, 1)
    got2p = from_rel(got3[: piece + SMALL], 3)
    got2q = from_rel(got1[piece + SMALL :], 1)
    over_x = swap(jnp.concatenate([got3[:piece], got1[:piece], got2p[:piece]], 0), x_bit)
    over_y = swap(jnp.concatenate([got3[piece + SMALL :], got1[piece + SMALL :], got2q], 0), y_bit)
    arrays = [bias_own, got3, got1, got2p, got2q, over_x, over_y]
    arrays += [swap(a, core_bit) for a in arrays[1:]]
    pieces = []
    for flip_core, base in ((0, 0), (1, 6)):
        pieces += [
            (1 + base, 0, 3, 0, 0, flip_core),
            (1 + base, piece + SMALL, 3, 1, 0, flip_core),
            (2 + base, 0, 1, 0, 0, flip_core),
            (2 + base, piece + SMALL, 1, 1, 0, flip_core),
            (3 + base, 0, 2, 0, 0, flip_core),
            (4 + base, 0, 2, 1, 0, flip_core),
        ]
        for i, rel in enumerate((3, 1, 2)):
            pieces.append((5 + base, i * piece, rel, 0, 1, flip_core))
            pieces.append((6 + base, i * piece, rel, 1, 1, flip_core))
    bias_at = {0: (0, 0), 3: (1, piece), 1: (2, piece), 2: (3, piece)}
    layout = Layout(len(arrays), pieces, bias_at, 0, units, units + qkv_cols)

    own_rows = pl.BlockSpec((length, model), lambda i, ids, *_: (ids[0], 0))

    dma = pltpu.SemaphoreType.DMA
    qkv, wo_all, resid, normed_two = pl.pallas_call(
        functools.partial(local_attn_kernel, layout),
        grid_spec=pltpu.PrefetchScalarGridSpec(
            num_scalar_prefetch=1,
            grid=(4,),
            in_specs=[own_rows, own_rows, ANY, whole(w_out), whole(wo_mine), whole(wo_other)]
            + [whole(a) for a in (row(b_out), gain_two, shift_two)]
            + [ANY] * layout.count,
            out_specs=[
                pl.BlockSpec((None, length, qkv_cols), lambda i, *_: (i, 0, 0)),
                pl.BlockSpec((None, width, model), lambda i, *_: (i, 0, 0)),
                pl.BlockSpec((length, model), lambda i, *_: (0, 0)),
                pl.BlockSpec((length, model), lambda i, *_: (0, 0)),
            ],
            scratch_shapes=[
                pltpu.VMEM((4, model, qkv_cols), bf16),
                pltpu.VMEM((4, SMALL, qkv_cols), bf16),
                pltpu.VMEM((length, model), f32),
                dma((4, 8)),
                dma((4,)),
                dma,
            ],
        ),
        out_shape=[
            sds((4, length, qkv_cols), bf16),
            sds((4, width, model), bf16),
            sds((length, model), f32),
            sds((length, model), bf16),
        ],
        compiler_params=params(),
        name="own_attention",
    )(ids, inputs, normed, wqkv, w_out, wo_mine, wo_other, row(b_out), gain_two, shift_two, *arrays)

    layer_out = pl.pallas_call(
        functools.partial(local_ffn_kernel, layout),
        grid_spec=pltpu.PrefetchScalarGridSpec(
            num_scalar_prefetch=1,
            grid=(4,),
            in_specs=[whole(resid), whole(normed_two), ANY, ANY, whole(row(b_down))]
            + [ANY] * layout.count,
            out_specs=pl.BlockSpec((length, model), lambda i, *_: (0, 0)),
            scratch_shapes=[
                pltpu.VMEM((4, model, units), bf16),
                pltpu.VMEM((4, units, model), bf16),
                pltpu.VMEM((4, SMALL, units), bf16),
                pltpu.VMEM((length, model), f32),
                dma((4, 8)),
                dma((4, 8)),
                dma((4,)),
                dma((2,)),
            ],
        ),
        out_shape=sds((length, model), bf16),
        compiler_params=params(),
        name="own_ffn",
    )(ids, resid, normed_two, w_up, w_down, row(b_down), *arrays)

    grad_inputs = pl.pallas_call(
        functools.partial(local_back_kernel, layout),
        grid_spec=pltpu.PrefetchScalarGridSpec(
            num_scalar_prefetch=2,
            grid=(4,),
            in_specs=[
                pl.BlockSpec((length, model), lambda i, span, ids: (ids[0], 0)),
                whole(gresid),
                whole(gb),
                pl.BlockSpec((None, length, qkv_cols), lambda i, *_: (i, 0, 0)),
                pl.BlockSpec((None, width, model), lambda i, *_: (i, 0, 0)),
                ANY,
                whole(gain_one),
            ]
            + [ANY] * layout.count,
            out_specs=pl.BlockSpec((length, model), lambda i, *_: (0, 0)),
            scratch_shapes=[
                pltpu.VMEM((4, model, qkv_cols), bf16),
                pltpu.VMEM((length, model), f32),
                dma((4, 8)),
                dma,
            ],
        ),
        out_shape=sds((length, model), bf16),
        compiler_params=params(),
        name="own_attention_back",
    )(span_table, ids, inputs, gresid, gb, qkv, wo_all, wqkv, gain_one, *arrays)

    return (
        layer_out,
        grad_inputs,
        norm_sums[0],
        norm_sums[1],
        grad_w_query,
        small[7, :width],
        grad_w_key,
        grad_w_value,
        small[8, :width],
        grad_w_out,
        small[2],
        small[3],
        small[4],
        grad_w_up,
        small[0],
        grad_w_down,
        small[1],
    )


def solution(mesh):
    return jax.shard_map(
        functools.partial(local, mesh.shape["dp"], mesh.shape["mp"]),
        mesh=mesh,
        in_specs=(
            P("dp", None),
            P("dp", None),
            P("dp", None),
            P(),
            P(),
            P(None, "mp"),
            P("mp"),
            P(None, "mp"),
            P(None, "mp"),
            P("mp"),
            P("mp", None),
            P(),
            P(),
            P(),
            P(None, "mp"),
            P("mp"),
            P("mp", None),
            P(),
        ),
        out_specs=(
            P(("dp", "mp"), None),
            P(("dp", "mp"), None),
            P(),
            P(),
            P(None, "mp"),
            P("mp"),
            P(None, "mp"),
            P(None, "mp"),
            P("mp"),
            P("mp", None),
            P(),
            P(),
            P(),
            P(None, "mp"),
            P("mp"),
            P("mp", None),
            P(),
        ),
        check_vma=False,
    )
```

time: 747 us -> 349 us (0.47); the launches traced: 738 us -> 348 us
  waiting for transfers between devices: 481 us -> 109 us
  starting transfers between devices: 0.42 us -> 112 us
  matrix products: 96.5 us -> 0 us
  Pallas kernels: 0 us -> 88.2 us
  other arithmetic: 59.8 us -> 2.75 us
  blocking collectives: 55.7 us -> 0 us
  between operations: 14.8 us -> 1.63 us
    psum x4 -> x0, waiting for transfers between devices: 481 us -> none  [the longest x1 176 us: local(): lax.psum(matmul(hidden_low, w_down).astype(jnp.bfloat16), 'mp')]
    ppermute x0 -> x44, starting transfers between devices: none -> 112 us  [the longest x19 91.1 us: from_rel(): lax.ppermute(value, 'mp', [(i, (i - rel) % mp_size) for i in range(mp_siz...]
    ppermute x0 -> x44, waiting for transfers between devices: none -> 109 us  [the longest x25 58.2 us: swap(): return lax.ppermute(value, 'dp', [(i, i ^ bits) for i in range(dp_size)])]
    dot_general x24 -> x0, matrix products: 96.5 us -> none  [the longest x6 34.6 us: matmul(): return jnp.dot(left, right, preferred_element_type=jnp.float32)]
    pallas_call x0 -> x15, Pallas kernels: none -> 88.2 us  [the longest x1 17.8 us: local(): pl.pallas_call(functools.partial(local_back_kernel, layout), grid_spec=pl...]
    psum x2 -> x0, blocking collectives: 55.7 us -> none  [the longest x1 40.5 us: local(): lax.psum((jnp.sum(grad_norm_one * unit_one_part, 0), jnp.sum(grad_norm_on...]
    convert_element_type x13 -> x0, other arithmetic: 30.8 us -> none  [the longest x1 8.69 us: local(): grad_branch = grad_resid.astype(bfloat)]
    reduce_sum x9 -> x0, other arithmetic: 23.3 us -> none  [the longest x2 6.32 us: normalize(): centered = values - jnp.mean(values, -1, keepdims=True)]
  transfers between devices with their start and end apart: 4 -> 44, of which waited for: 4 -> 22; matrix products, arithmetic and copies ran while one was open for 7% -> 5% of each run, Pallas kernels for 0% -> 12%
where the time goes in v1:
time: 349 us; the launch traced here: 348 us
  starting transfers between devices  112 us (32%)
  waiting for transfers between devices  109 us (31%)
  Pallas kernels  88.2 us (25%)
  local copies, waits for them, and re-layouts  34.9 us (10%)
    ppermute x19, starting transfers between devices, from_rel(): lax.ppermute(value, 'mp', [(i, (i - rel) % mp_size) for i in range(mp_siz...  91.1 us
    ppermute x25, waiting for transfers between devices, swap(): return lax.ppermute(value, 'dp', [(i, i ^ bits) for i in range(dp_size)])  58.2 us
    ppermute x19, waiting for transfers between devices, from_rel(): lax.ppermute(value, 'mp', [(i, (i - rel) % mp_size) for i in range(mp_siz...  50.5 us
    unnamed x115, local copies, waits for them, and re-layouts  26.7 us
    ppermute x25, starting transfers between devices, swap(): return lax.ppermute(value, 'dp', [(i, i ^ bits) for i in range(dp_size)])  20.6 us
    pallas_call x1, Pallas kernels, local(): pl.pallas_call(functools.partial(local_back_kernel, layout), grid_spec=pl...  17.8 us
    pallas_call x1, Pallas kernels, local(): pl.pallas_call(functools.partial(local_attn_kernel, layout), grid_spec=pl...  15.8 us
    pallas_call x1, Pallas kernels, local(): pl.pallas_call(attn_kernel, grid_spec=pltpu.PrefetchScalarGridSpec(num_sc...  13.9 us
  transfers between devices with their start and end apart: 44, of which 22 were waited for; matrix products, arithmetic and copies ran while one was open for 5% of the time, Pallas kernels for 12%

profile of v1, /device:TPU:0, one launch (start us, length us, event | category | flops | bytes accessed | tf_op | source)
XLA Modules:
  0.0 348.0 jit_solution(4503273785935931766)
XLA Ops:
  2.3 3.0 collective-permute-start.2
  5.3 2.6 collective-permute-start.1
  19.9 11.9 %windows_forward.1 = (bf16[2048,768]{1,0:T(8,128)(2,1)}, bf16[512,768]{1,0:T(8,128)(2,1)S(1)}, bf16[512,768]{1,0:T(8,128)(2,1)S(1)}, bf16[512,768]{1,0:T(8,128)(...) custom-call(s32[4,2]{1,0:T(4,128)S(1)} %copy.35.span_ref, ...), custom_call_target="tpu_custom_call" | custom-call | tf_op jit(solution)/shard_map/windows_forward/pallas_call | solution.py:558
  37.1 21.4 %collective-permute-start.18 = (bf16[512,192]{1,0:T(8,128)(2,1)}, bf16[512,192]{1,0:T(8,128)(2,1)S(1)}, u32[]{:S(2)}, u32[]{:S(2)}) collective-permute-start(bf16[512,192]{1,0:T(8,128)(2,1)} %get-tuple-element.61.m0_ref.mw_ref), channel_id=1, source_target_pairs={{0,1},{1,2},{2,3},{3,0},{4,5},{5,6},{6,7},{7,4},{8,9},{9,10},{10,1... | collective-permute-start | bytes 589832 | tf_op jit(solution)/shard_map/ppermute | solution.py:530
  58.5 3.3 collective-permute-start.17
  61.9 6.8 %collective-permute-done.18.m3_ref = bf16[512,192]{1,0:T(8,128)(2,1)S(1)} collective-permute-done((bf16[512,192]{1,0:T(8,128)(2,1)}, bf16[512,192]{1,0:T(8,128)(2,1)S(1)}, u32[]{:S(2)}, u32[]{:S(2)}) %collective-permute-start.18) | collective-permute-done | bytes 196640 | tf_op jit(solution)/shard_map/ppermute | solution.py:530
  68.7 11.0 %collective-permute-done.17.m2_ref = bf16[512,192]{1,0:T(8,128)(2,1)S(1)} collective-permute-done((bf16[512,192]{1,0:T(8,128)(2,1)}, bf16[512,192]{1,0:T(8,128)(2,1)S(1)}, u32[]{:S(2)}, u32[]{:S(2)}) %collective-permute-start.17) | collective-permute-done | bytes 196640 | tf_op jit(solution)/shard_map/ppermute | solution.py:530
  82.1 8.9 %windows_ffn.1 = (bf16[768,768]{1,0:T(8,128)(2,1)}, bf16[768,768]{1,0:T(8,128)(2,1)}, bf16[128,768]{1,0:T(8,128)(2,1)S(1)}, bf16[128,768]{1,0:T(8,128)(2,1)S(1)}...) custom-call(s32[6]{0:T(128)S(1)} %stack.35.ids_ref, ...), custom_call_target="tpu_custom_call" | custom-call | tf_op jit(solution)/shard_map/windows_ffn/pallas_call | solution.py:593
  91.1 6.1 %collective-permute-start.19 = (bf16[128,768]{1,0:T(8,128)(2,1)S(1)}, bf16[128,768]{1,0:T(8,128)(2,1)S(1)}, u32[]{:S(2)}, u32[]{:S(2)}) collective-permute-start(bf16[128,768]{1,0:T(8,128)(2,1)S(1)} %get-tuple-element.65), channel_id=1, source_target_pairs={{0,1},{1,2},{2,3},{3,0},{4,5},{5,6},{6,7},{7,4},{8,9},{9,10},{10,1... | collective-permute-start | bytes 589832 | tf_op jit(solution)/shard_map/ppermute | solution.py:530
  99.6 2.8 collective-permute-done.19.p1_ref
  102.5 8.0 %collective-permute-done.20.p2_ref = bf16[128,768]{1,0:T(8,128)(2,1)S(1)} collective-permute-done((bf16[128,768]{1,0:T(8,128)(2,1)S(1)}, bf16[128,768]{1,0:T(8,128)(2,1)S(1)}, u32[]{:S(2)}, u32[]{:S(2)}) %collective-permute-start.20) | collective-permute-done | bytes 196640 | tf_op jit(solution)/shard_map/ppermute | solution.py:530
  111.5 27.6 %collective-permute-start.24 = (bf16[144,768]{1,0:T(8,128)(2,1)S(1)}, bf16[144,768]{1,0:T(8,128)(2,1)S(1)}, u32[]{:S(2)}, u32[]{:S(2)}) collective-permute-start(bf16[144,768]{1,0:T(8,128)(2,1)S(1)} %get-tuple-element.71.gb_ref.g0_ref), channel_id=1, source_target_pairs={{0,1},{1,2},{2,3},{3,0},{4,5},{5,6},{6,7},{7,4},{8,9},{9,10},{10,1... | collective-permute-start | bytes 663560 | tf_op jit(solution)/shard_map/ppermute | solution.py:530
  147.5 4.3 %collective-permute-done.23.g2_ref = bf16[144,768]{1,0:T(8,128)(2,1)S(1)} collective-permute-done((bf16[144,768]{1,0:T(8,128)(2,1)S(1)}, bf16[144,768]{1,0:T(8,128)(2,1)S(1)}, u32[]{:S(2)}, u32[]{:S(2)}) %collective-permute-start.23) | collective-permute-done | bytes 221216 | tf_op jit(solution)/shard_map/ppermute | solution.py:530
  151.8 2.7 collective-permute-done.22.g1_ref
  154.5 13.9 %windows_attention_back.1 = (bf16[400,768]{1,0:T(8,128)(2,1)S(1)}, bf16[400,768]{1,0:T(8,128)(2,1)S(1)}) custom-call(s32[6]{0:T(128)S(1)} %stack.35.ids_ref, bf16[144,768]{1,0:T(8,128)(2,1)S(1)} %get-tuple-element.71.gb_ref.g0_ref, bf16[144,768]{1,0:T(8,128)(2,1)S(1)} %collective-permute-done.22.g1_ref, bf16[144,768]{1,0:T(8,128)(2,1)S(1)} %collective-permute-done.23.g2_ref, ...), custom_call_target="tpu_custom_call" | custom-call | tf_op jit(solution)/shard_map/windows_attention_back/pallas_call | solution.py:681
  170.2 2.7 collective-permute-done.6.refs_3_
  177.5 6.4 %collective-permute-done.37.a_ref = bf16[192,768]{1,0:T(8,128)(2,1)S(1)} collective-permute-done((bf16[192,768]{1,0:T(8,128)(2,1)S(1)}, bf16[192,768]{1,0:T(8,128)(2,1)S(1)}, u32[]{:S(2)}, u32[]{:S(2)}) %collective-permute-start.37) | collective-permute-done | bytes 294944 | tf_op jit(solution)/shard_map/ppermute | solution.py:536
  185.3 25.9 %collective-permute-done.38.b_ref = bf16[192,768]{1,0:T(8,128)(2,1)S(1)} collective-permute-done((bf16[192,768]{1,0:T(8,128)(2,1)S(1)}, bf16[192,768]{1,0:T(8,128)(2,1)S(1)}, u32[]{:S(2)}, u32[]{:S(2)}) %collective-permute-start.38) | collective-permute-done | bytes 294944 | tf_op jit(solution)/shard_map/ppermute | solution.py:536
  211.4 2.5 collective-permute-start.42
  215.7 8.2 %collective-permute-done.42.refs_3_ = bf16[192,768]{1,0:T(8,128)(2,1)S(1)} collective-permute-done((bf16[192,768]{1,0:T(8,128)(2,1)S(1)}, bf16[192,768]{1,0:T(8,128)(2,1)S(1)}, u32[]{:S(2)}, u32[]{:S(2)}) %collective-permute-start.42) | collective-permute-done | bytes 294944 | tf_op jit(solution)/shard_map/ppermute | solution.py:536
  225.4 2.7 collective-permute-done.41.refs_2_
  229.1 2.6 collective-permute-start.28
  232.4 5.0 %collective-permute-done.27.b_ref = bf16[112,768]{1,0:T(8,128)(2,1)S(1)} collective-permute-done((bf16[112,768]{1,0:T(8,128)(2,1)S(1)}, bf16[112,768]{1,0:T(8,128)(2,1)S(1)}, u32[]{:S(2)}, u32[]{:S(2)}) %collective-permute-start.27) | collective-permute-done | bytes 172064 | tf_op jit(solution)/shard_map/ppermute | solution.py:536
  240.0 3.7 %collective-permute-done.34.refs_3_ = bf16[96,768]{1,0:T(8,128)(2,1)S(1)} collective-permute-done((bf16[96,768]{1,0:T(8,128)(2,1)S(1)}, bf16[96,768]{1,0:T(8,128)(2,1)S(1)}, u32[]{:S(2)}, u32[]{:S(2)}) %collective-permute-start.34) | collective-permute-done | bytes 147488 | tf_op jit(solution)/shard_map/ppermute | solution.py:536
  245.2 3.6 %collective-permute-done.32.refs_1_ = bf16[96,768]{1,0:T(8,128)(2,1)S(1)} collective-permute-done((bf16[96,768]{1,0:T(8,128)(2,1)S(1)}, bf16[96,768]{1,0:T(8,128)(2,1)S(1)}, u32[]{:S(2)}, u32[]{:S(2)}) %collective-permute-start.32) | collective-permute-done | bytes 147488 | tf_op jit(solution)/shard_map/ppermute | solution.py:536
  253.5 13.6 %collective-permute-start.31 = (f32[2,768]{1,0:T(2,128)S(1)}, f32[2,768]{1,0:T(2,128)S(1)}, u32[]{:S(2)}, u32[]{:S(2)}) collective-permute-start(f32[2,768]{1,0:T(2,128)S(1)} %slice.55), channel_id=1, source_target_pairs={{0,1},{1,2},{2,3},{3,0},{4,5},{5,6},{6,7},{7,4},{8,9},{9,10},{10,1... | collective-permute-start | bytes 18440 | tf_op jit(solution)/shard_map/ppermute | solution.py:530
  267.1 4.4 %collective-permute-done.31 = f32[2,768]{1,0:T(2,128)S(1)} collective-permute-done((f32[2,768]{1,0:T(2,128)S(1)}, f32[2,768]{1,0:T(2,128)S(1)}, u32[]{:S(2)}, u32[]{:S(2)}) %collective-permute-start.31) | collective-permute-done | bytes 6176 | tf_op jit(solution)/shard_map/ppermute | solution.py:530
  271.8 4.2 %collective-permute-done.30 = f32[2,768]{1,0:T(2,128)S(1)} collective-permute-done((f32[2,768]{1,0:T(2,128)S(1)}, f32[2,768]{1,0:T(2,128)S(1)}, u32[]{:S(2)}, u32[]{:S(2)}) %collective-permute-start.30) | collective-permute-done | bytes 6176 | tf_op jit(solution)/shard_map/ppermute | solution.py:530
  297.2 3.3 ffn_gradients.1
  301.4 15.8 %own_attention.1 = (bf16[4,512,640]{2,1,0:T(8,128)(2,1)}, bf16[4,192,768]{2,1,0:T(8,128)(2,1)}, f32[512,768]{1,0:T(8,128)}, bf16[512,768]{1,0:T(8,128)(2,1)S(1)}) custom-call(s32[6]{0:T(128)S(1)} %stack.35.ids_ref, bf16[2048,768]{1,0:T(8,128)(2,1)} %x_ref.5, bf16[2048,768]{1,0:T(8,128)(2,1)} %get-tuple-element.58.normed_ref, bf16[768,640]{1,0:T(8,128)(2,1)} %copy-done.39, ...), custom_call_target="tpu_custom_call" | custom-call | tf_op jit(solution)/shard_map/own_attention/pallas_call | solution.py:768
  318.4 17.8 %own_attention_back.1 = bf16[512,768]{1,0:T(8,128)(2,1)} custom-call(s32[4,2]{1,0:T(4,128)S(1)} %copy.35.span_ref, s32[6]{0:T(128)S(1)} %stack.35.ids_ref, bf16[2048,768]{1,0:T(8,128)(2,1)} %x_ref.5, f32[128,768]{1,0:T(8,128)S(1)} %copy-done.36, bf16[144,768]{1,0:T(8,128)(2,1)S(1)} %copy-done.25, bf16[4,512,640]{2,1,0:T(8,128)(2,1)} %get-tuple-element.72.qkv_ref, ...), custom_call_target="tpu_custom_call" | custom-call | tf_op jit(solution)/shard_map/own_attention_back/pallas_call | solution.py:825
  336.2 11.6 %own_ffn.1 = bf16[512,768]{1,0:T(8,128)(2,1)} custom-call(s32[6]{0:T(128)S(1)} %stack.35.ids_ref, f32[512,768]{1,0:T(8,128)} %get-tuple-element.59.resid_ref, bf16[512,768]{1,0:T(8,128)(2,1)S(1)} %get-tuple-element.60.normed_ref, bf16[768,768]{1,0:T(8,128)(2,1)} %wup_ref.3, bf16[768,768]{1,0:T(8,128)(2,1)} %wdown_ref.3, ...), custom_call_target="tpu_custom_call" | custom-call | tf_op jit(solution)/shard_map/own_ffn/pallas_call | solution.py:801
  (222 shorter events, 78.0 us)
Async XLA Ops:
  2.3 15.4 %collective-permute-start.2 = (bf16[96,768]{1,0:T(8,128)(2,1)}, bf16[96,768]{1,0:T(8,128)(2,1)S(1)}, u32[]{:S(2)}, u32[]{:S(2)}) collective-permute-start(bf16[96,768]{1,0:T(8,128)(2,1)} %constant_dynamic-slice_fusion.6), channel_id=1, source_target_pairs={{0,1},{1,2},{2,3},{3,0},{4,5},{5,6},{6,7},{7,4},{8,9},{9,10},{10,1... | collective-permute-start | bytes 442376 | tf_op jit(solution)/shard_map/ppermute | solution.py:530
  5.3 12.5 %collective-permute-start.1 = (bf16[96,768]{1,0:T(8,128)(2,1)}, bf16[96,768]{1,0:T(8,128)(2,1)S(1)}, u32[]{:S(2)}, u32[]{:S(2)}) collective-permute-start(bf16[96,768]{1,0:T(8,128)(2,1)} %constant_dynamic-slice_fusion.6), channel_id=1, source_target_pairs={{0,2},{1,3},{2,0},{3,1},{4,6},{5,7},{6,4},{7,5},{8,10},{9,11},{10,... | collective-permute-start | bytes 442376 | tf_op jit(solution)/shard_map/ppermute | solution.py:530
  17.2 121.9 %collective-permute-start.5 = (bf16[208,2176]{1,0:T(8,128)(2,1)}, bf16[208,2176]{1,0:T(8,128)(2,1)S(1)}, u32[]{:S(2)}, u32[]{:S(2)}) collective-permute-start(bf16[208,2176]{1,0:T(8,128)(2,1)} %maximum_maximum_fusion.1), channel_id=1, source_target_pairs={{0,3},{1,0},{2,1},{3,2},{4,7},{5,4},{6,5},{7,6},{8,11},{9,8},{10,9... | collective-permute-start | bytes 2715656 | tf_op jit(solution)/shard_map/ppermute | solution.py:530
  19.5 60.2 %collective-permute-start.3 = (bf16[3,96,768]{2,1,0:T(8,128)(2,1)S(1)}, bf16[3,96,768]{2,1,0:T(8,128)(2,1)S(1)}, u32[]{:S(2)}, u32[]{:S(2)}) collective-permute-start(bf16[3,96,768]{2,1,0:T(8,128)(2,1)S(1)} %pad_maximum_fusion.2.wo_mine_ref), channel_id=1, source_target_pairs={{0,4},{4,0},{8,12},{12,8},{16,20},{20,16},{24,28},{28,24},{1,5},{5... | collective-permute-start | bytes 1327112 | tf_op jit(solution)/shard_map/ppermute | solution.py:536
  37.1 31.6 %collective-permute-start.18 = (bf16[512,192]{1,0:T(8,128)(2,1)}, bf16[512,192]{1,0:T(8,128)(2,1)S(1)}, u32[]{:S(2)}, u32[]{:S(2)}) collective-permute-start(bf16[512,192]{1,0:T(8,128)(2,1)} %get-tuple-element.61.m0_ref.mw_ref), channel_id=1, source_target_pairs={{0,1},{1,2},{2,3},{3,0},{4,5},{5,6},{6,7},{7,4},{8,9},{9,10},{10,1... | collective-permute-start | bytes 589832 | tf_op jit(solution)/shard_map/ppermute | solution.py:530
  58.5 21.2 %collective-permute-start.17 = (bf16[512,192]{1,0:T(8,128)(2,1)}, bf16[512,192]{1,0:T(8,128)(2,1)S(1)}, u32[]{:S(2)}, u32[]{:S(2)}) collective-permute-start(bf16[512,192]{1,0:T(8,128)(2,1)} %get-tuple-element.61.m0_ref.mw_ref), channel_id=1, source_target_pairs={{0,2},{1,3},{2,0},{3,1},{4,6},{5,7},{6,4},{7,5},{8,10},{9,11},{10,... | collective-permute-start | bytes 589832 | tf_op jit(solution)/shard_map/ppermute | solution.py:530
  61.8 17.9 %collective-permute-start.16 = (bf16[512,192]{1,0:T(8,128)(2,1)}, bf16[512,192]{1,0:T(8,128)(2,1)S(1)}, u32[]{:S(2)}, u32[]{:S(2)}) collective-permute-start(bf16[512,192]{1,0:T(8,128)(2,1)} %get-tuple-element.61.m0_ref.mw_ref), channel_id=1, source_target_pairs={{0,3},{1,0},{2,1},{3,2},{4,7},{5,4},{6,5},{7,6},{8,11},{9,8},{10,9... | collective-permute-start | bytes 589832 | tf_op jit(solution)/shard_map/ppermute | solution.py:530
  97.2 13.3 %collective-permute-start.20 = (bf16[128,768]{1,0:T(8,128)(2,1)S(1)}, bf16[128,768]{1,0:T(8,128)(2,1)S(1)}, u32[]{:S(2)}, u32[]{:S(2)}) collective-permute-start(bf16[128,768]{1,0:T(8,128)(2,1)S(1)} %get-tuple-element.66), channel_id=1, source_target_pairs={{0,2},{1,3},{2,0},{3,1},{4,6},{5,7},{6,4},{7,5},{8,10},{9,11},{10,... | collective-permute-start | bytes 589832 | tf_op jit(solution)/shard_map/ppermute | solution.py:530
  97.2 13.8 %collective-permute-start.21 = (bf16[128,768]{1,0:T(8,128)(2,1)S(1)}, bf16[128,768]{1,0:T(8,128)(2,1)S(1)}, u32[]{:S(2)}, u32[]{:S(2)}) collective-permute-start(bf16[128,768]{1,0:T(8,128)(2,1)S(1)} %get-tuple-element.67), channel_id=1, source_target_pairs={{0,3},{1,0},{2,1},{3,2},{4,7},{5,4},{6,5},{7,6},{8,11},{9,8},{10,9... | collective-permute-start | bytes 589832 | tf_op jit(solution)/shard_map/ppermute | solution.py:530
  99.6 42.0 %collective-permute-start.4 = (bf16[208,2176]{1,0:T(8,128)(2,1)}, bf16[208,2176]{1,0:T(8,128)(2,1)S(1)}, u32[]{:S(2)}, u32[]{:S(2)}) collective-permute-start(bf16[208,2176]{1,0:T(8,128)(2,1)} %maximum_maximum_fusion.1), channel_id=1, source_target_pairs={{0,1},{1,2},{2,3},{3,0},{4,5},{5,6},{6,7},{7,4},{8,9},{9,10},{10,1... | collective-permute-start | bytes 2715656 | tf_op jit(solution)/shard_map/ppermute | solution.py:530
  102.5 70.5 %collective-permute-start.36 = (bf16[768,768]{1,0:T(8,128)(2,1)}, bf16[768,768]{1,0:T(8,128)(2,1)S(1)}, u32[]{:S(2)}, u32[]{:S(2)}) collective-permute-start(bf16[768,768]{1,0:T(8,128)(2,1)} %get-tuple-element.92), channel_id=1, source_target_pairs={{0,4},{4,0},{8,12},{12,8},{16,20},{20,16},{24,28},{28,24},{1,5},{5... | collective-permute-start | bytes 3538952 | tf_op jit(solution)/shard_map/ppermute | solution.py:536
  111.5 33.4 %collective-permute-start.24 = (bf16[144,768]{1,0:T(8,128)(2,1)S(1)}, bf16[144,768]{1,0:T(8,128)(2,1)S(1)}, u32[]{:S(2)}, u32[]{:S(2)}) collective-permute-start(bf16[144,768]{1,0:T(8,128)(2,1)S(1)} %get-tuple-element.71.gb_ref.g0_ref), channel_id=1, source_target_pairs={{0,1},{1,2},{2,3},{3,0},{4,5},{5,6},{6,7},{7,4},{8,9},{9,10},{10,1... | collective-permute-start | bytes 663560 | tf_op jit(solution)/shard_map/ppermute | solution.py:530
  139.1 12.6 %collective-permute-start.23 = (bf16[144,768]{1,0:T(8,128)(2,1)S(1)}, bf16[144,768]{1,0:T(8,128)(2,1)S(1)}, u32[]{:S(2)}, u32[]{:S(2)}) collective-permute-start(bf16[144,768]{1,0:T(8,128)(2,1)S(1)} %get-tuple-element.71.gb_ref.g0_ref), channel_id=1, source_target_pairs={{0,2},{1,3},{2,0},{3,1},{4,6},{5,7},{6,4},{7,5},{8,10},{9,11},{10,... | collective-permute-start | bytes 663560 | tf_op jit(solution)/shard_map/ppermute | solution.py:530
  139.1 15.4 %collective-permute-start.22 = (bf16[144,768]{1,0:T(8,128)(2,1)S(1)}, bf16[144,768]{1,0:T(8,128)(2,1)S(1)}, u32[]{:S(2)}, u32[]{:S(2)}) collective-permute-start(bf16[144,768]{1,0:T(8,128)(2,1)S(1)} %get-tuple-element.71.gb_ref.g0_ref), channel_id=1, source_target_pairs={{0,3},{1,0},{2,1},{3,2},{4,7},{5,4},{6,5},{7,6},{8,11},{9,8},{10,9... | collective-permute-start | bytes 663560 | tf_op jit(solution)/shard_map/ppermute | solution.py:530
  141.7 26.9 %collective-permute-start.7 = (bf16[96,2176]{1,0:T(8,128)(2,1)S(1)}, bf16[96,2176]{1,0:T(8,128)(2,1)S(1)}, u32[]{:S(2)}, u32[]{:S(2)}) collective-permute-start(bf16[96,2176]{1,0:T(8,128)(2,1)S(1)} %get-tuple-element.132), channel_id=1, source_target_pairs={{0,3},{1,0},{2,1},{3,2},{4,7},{5,4},{6,5},{7,6},{8,11},{9,8},{10,9... | collective-permute-start | bytes 1253384 | tf_op jit(solution)/shard_map/ppermute | solution.py:530
  144.9 28.0 %collective-permute-start.6 = (bf16[112,2176]{1,0:T(8,128)(2,1)S(1)}, bf16[112,2176]{1,0:T(8,128)(2,1)S(1)}, u32[]{:S(2)}, u32[]{:S(2)}) collective-permute-start(bf16[112,2176]{1,0:T(8,128)(2,1)S(1)} %slice.65), channel_id=1, source_target_pairs={{0,1},{1,2},{2,3},{3,0},{4,5},{5,6},{6,7},{7,4},{8,9},{9,10},{10,1... | collective-permute-start | bytes 1462280 | tf_op jit(solution)/shard_map/ppermute | solution.py:530
  168.4 46.0 %collective-permute-start.25 = (bf16[400,768]{1,0:T(8,128)(2,1)S(1)}, bf16[400,768]{1,0:T(8,128)(2,1)S(1)}, u32[]{:S(2)}, u32[]{:S(2)}) collective-permute-start(bf16[400,768]{1,0:T(8,128)(2,1)S(1)} %get-tuple-element.80), channel_id=1, source_target_pairs={{0,4},{4,0},{8,12},{12,8},{16,20},{20,16},{24,28},{28,24},{1,5},{5... | collective-permute-start | bytes 1843208 | tf_op jit(solution)/shard_map/ppermute | solution.py:536
  168.6 81.4 %collective-permute-start.9 = (bf16[288,2176]{1,0:T(8,128)(2,1)S(1)}, bf16[288,2176]{1,0:T(8,128)(2,1)}, u32[]{:S(2)}, u32[]{:S(2)}) collective-permute-start(bf16[288,2176]{1,0:T(8,128)(2,1)S(1)} %pad_maximum_fusion.1), channel_id=1, source_target_pairs={{0,16},{4,20},{8,24},{12,28},{16,0},{20,4},{24,8},{28,12},{1,17},{... | collective-permute-start | bytes 3760136 | tf_op jit(solution)/shard_map/ppermute | solution.py:536
  175.4 35.9 %collective-permute-start.38 = (bf16[192,768]{1,0:T(8,128)(2,1)S(1)}, bf16[192,768]{1,0:T(8,128)(2,1)S(1)}, u32[]{:S(2)}, u32[]{:S(2)}) collective-permute-start(bf16[192,768]{1,0:T(8,128)(2,1)S(1)} %get-tuple-element.95), channel_id=1, source_target_pairs={{0,16},{4,20},{8,24},{12,28},{16,0},{20,4},{24,8},{28,12},{1,17},{... | collective-permute-start | bytes 884744 | tf_op jit(solution)/shard_map/ppermute | solution.py:536
  176.9 34.4 %collective-permute-start.39 = (bf16[192,768]{1,0:T(8,128)(2,1)S(1)}, bf16[192,768]{1,0:T(8,128)(2,1)S(1)}, u32[]{:S(2)}, u32[]{:S(2)}) collective-permute-start(bf16[192,768]{1,0:T(8,128)(2,1)S(1)} %get-tuple-element.96), channel_id=1, source_target_pairs={{0,24},{4,28},{8,16},{12,20},{16,8},{20,12},{24,0},{28,4},{1,25},{... | collective-permute-start | bytes 884744 | tf_op jit(solution)/shard_map/ppermute | solution.py:536
  183.8 66.3 %collective-permute-start.8 = (bf16[288,2176]{1,0:T(8,128)(2,1)S(1)}, bf16[288,2176]{1,0:T(8,128)(2,1)}, u32[]{:S(2)}, u32[]{:S(2)}) collective-permute-start(bf16[288,2176]{1,0:T(8,128)(2,1)S(1)} %pad_maximum_fusion), channel_id=1, source_target_pairs={{0,8},{4,12},{8,0},{12,4},{16,24},{20,28},{24,16},{28,20},{1,9},{5... | collective-permute-start | bytes 3760136 | tf_op jit(solution)/shard_map/ppermute | solution.py:536
  211.4 12.4 %collective-permute-start.42 = (bf16[192,768]{1,0:T(8,128)(2,1)S(1)}, bf16[192,768]{1,0:T(8,128)(2,1)S(1)}, u32[]{:S(2)}, u32[]{:S(2)}) collective-permute-start(bf16[192,768]{1,0:T(8,128)(2,1)S(1)} %ffn_total.1.refs_0_), channel_id=1, source_target_pairs={{0,24},{4,28},{8,16},{12,20},{16,8},{20,12},{24,0},{28,4},{1,25},{... | collective-permute-start | bytes 884744 | tf_op jit(solution)/shard_map/ppermute | solution.py:536
  213.9 14.1 %collective-permute-start.41 = (bf16[192,768]{1,0:T(8,128)(2,1)S(1)}, bf16[192,768]{1,0:T(8,128)(2,1)S(1)}, u32[]{:S(2)}, u32[]{:S(2)}) collective-permute-start(bf16[192,768]{1,0:T(8,128)(2,1)S(1)} %ffn_total.1.refs_0_), channel_id=1, source_target_pairs={{0,16},{4,20},{8,24},{12,28},{16,0},{20,4},{24,8},{28,12},{1,17},{... | collective-permute-start | bytes 884744 | tf_op jit(solution)/shard_map/ppermute | solution.py:536
  214.4 14.7 %collective-permute-start.40 = (bf16[192,768]{1,0:T(8,128)(2,1)S(1)}, bf16[192,768]{1,0:T(8,128)(2,1)S(1)}, u32[]{:S(2)}, u32[]{:S(2)}) collective-permute-start(bf16[192,768]{1,0:T(8,128)(2,1)S(1)} %ffn_total.1.refs_0_), channel_id=1, source_target_pairs={{0,8},{4,12},{8,0},{12,4},{16,24},{20,28},{24,16},{28,20},{1,9},{5... | collective-permute-start | bytes 884744 | tf_op jit(solution)/shard_map/ppermute | solution.py:536
  232.3 48.5 %collective-permute-start.43 = (bf16[768,768]{1,0:T(8,128)(2,1)S(1)}, bf16[768,768]{1,0:T(8,128)(2,1)S(1)}, u32[]{:S(2)}, u32[]{:S(2)}) collective-permute-start(bf16[768,768]{1,0:T(8,128)(2,1)S(1)} %ffn_place.1.mine_ref), channel_id=1, source_target_pairs={{0,4},{4,0},{8,12},{12,8},{16,20},{20,16},{24,28},{28,24},{1,5},{5... | collective-permute-start | bytes 3538952 | tf_op jit(solution)/shard_map/ppermute | solution.py:536
  249.4 30.2 %collective-permute-start.35 = (bf16[384,768]{1,0:T(8,128)(2,1)S(1)}, bf16[384,768]{1,0:T(8,128)(2,1)S(1)}, u32[]{:S(2)}, u32[]{:S(2)}) collective-permute-start(bf16[384,768]{1,0:T(8,128)(2,1)S(1)} %att_place.1.mine_ref), channel_id=1, source_target_pairs={{0,4},{4,0},{8,12},{12,8},{16,20},{20,16},{24,28},{28,24},{1,5},{5... | collective-permute-start | bytes 1769480 | tf_op jit(solution)/shard_map/ppermute | solution.py:536
  250.0 50.5 %collective-permute-start.15 = (bf16[288,2176]{1,0:T(8,128)(2,1)}, bf16[288,2176]{1,0:T(8,128)(2,1)}, u32[]{:S(2)}, u32[]{:S(2)}) collective-permute-start(bf16[288,2176]{1,0:T(8,128)(2,1)} %collective-permute-done.9.refs_6_), channel_id=1, source_target_pairs={{0,4},{4,0},{8,12},{12,8},{16,20},{20,16},{24,28},{28,24},{1,5},{5... | collective-permute-start | bytes 3760136 | tf_op jit(solution)/shard_map/ppermute | solution.py:536
  250.1 50.4 %collective-permute-start.14 = (bf16[288,2176]{1,0:T(8,128)(2,1)}, bf16[288,2176]{1,0:T(8,128)(2,1)}, u32[]{:S(2)}, u32[]{:S(2)}) collective-permute-start(bf16[288,2176]{1,0:T(8,128)(2,1)} %collective-permute-done.8.refs_5_), channel_id=1, source_target_pairs={{0,4},{4,0},{8,12},{12,8},{16,20},{20,16},{24,28},{28,24},{1,5},{5... | collective-permute-start | bytes 3760136 | tf_op jit(solution)/shard_map/ppermute | solution.py:536
  253.5 18.0 %collective-permute-start.31 = (f32[2,768]{1,0:T(2,128)S(1)}, f32[2,768]{1,0:T(2,128)S(1)}, u32[]{:S(2)}, u32[]{:S(2)}) collective-permute-start(f32[2,768]{1,0:T(2,128)S(1)} %slice.55), channel_id=1, source_target_pairs={{0,1},{1,2},{2,3},{3,0},{4,5},{5,6},{6,7},{7,4},{8,9},{9,10},{10,1... | collective-permute-start | bytes 18440 | tf_op jit(solution)/shard_map/ppermute | solution.py:530
  279.6 20.8 %collective-permute-start.11 = (bf16[208,2176]{1,0:T(8,128)(2,1)S(1)}, bf16[208,2176]{1,0:T(8,128)(2,1)S(1)}, u32[]{:S(2)}, u32[]{:S(2)}) collective-permute-start(bf16[208,2176]{1,0:T(8,128)(2,1)S(1)} %collective-permute-done.5.refs_2_), channel_id=1, source_target_pairs={{0,4},{4,0},{8,12},{12,8},{16,20},{20,16},{24,28},{28,24},{1,5},{5... | collective-permute-start | bytes 2715656 | tf_op jit(solution)/shard_map/ppermute | solution.py:536
  279.6 20.8 %collective-permute-start.10 = (bf16[208,2176]{1,0:T(8,128)(2,1)S(1)}, bf16[208,2176]{1,0:T(8,128)(2,1)}, u32[]{:S(2)}, u32[]{:S(2)}) collective-permute-start(bf16[208,2176]{1,0:T(8,128)(2,1)S(1)} %collective-permute-done.4.refs_1_), channel_id=1, source_target_pairs={{0,4},{4,0},{8,12},{12,8},{16,20},{20,16},{24,28},{28,24},{1,5},{5... | collective-permute-start | bytes 2715656 | tf_op jit(solution)/shard_map/ppermute | solution.py:536
  281.8 18.7 %collective-permute-start.12 = (bf16[112,2176]{1,0:T(8,128)(2,1)S(1)}, bf16[112,2176]{1,0:T(8,128)(2,1)}, u32[]{:S(2)}, u32[]{:S(2)}) collective-permute-start(bf16[112,2176]{1,0:T(8,128)(2,1)S(1)} %collective-permute-done.6.refs_3_), channel_id=1, source_target_pairs={{0,4},{4,0},{8,12},{12,8},{16,20},{20,16},{24,28},{28,24},{1,5},{5... | collective-permute-start | bytes 1462280 | tf_op jit(solution)/shard_map/ppermute | solution.py:536
  (66 other events, 1040.6 us)
